TPU v7x, 32 devices: a whole 2x2x4 slice. The times are simulated.
32 devices in a mesh: blk: 16 (over z, x, core), fiber: 2 (over y).
Axes of the slice: x: 2, y: 2, z: 4, core: 2. Of those that a mesh axis runs over, the one named last changes fastest.
Arguments:
- queries: bfloat16 [8192, 256], P(('blk', 'fiber')), may hold values from -6 to 6
- keys: bfloat16 [8192, 256], P(('blk', 'fiber')), may hold values from -6 to 6
- values: bfloat16 [8192, 256], P(('blk', 'fiber')), may hold values from -6 to 6
- tiles: int32 [16, 2, 4, 4], P('blk', 'fiber'), may hold values from -1 to 7, as said below
- edges: bfloat16 [16, 2, 4, 4, 128, 128], P('blk', 'fiber'), may hold values from 0.05 to 2, as said below
Outputs:
- attended: bfloat16 [8192, 256], P(('blk', 'fiber'))
Inputs may be any that keep to these rules, and one draw needn't show every extreme that they name: tiles[b, f, s, :] lists the occupied tiles between query block b and key subblock f of block (b - s) mod 16: distinct numbers r * 2 + c (row tile r, column tile c) in the first slots, then -1 in the slots left over. Each list holds at least one tile, and in every draw some list is full. edges[c, f, s, k] holds the edge values of the tile in slot k of the list tiles[(c + s) mod 16, f, s]; slots marked -1 there hold values of no edge.
All inputs are finite; a program needn't handle non-finite values.
Results may differ from a plain program's by a relative error of at most 0.0049.
Values may be sent and summed in bfloat16 or wider, within the bound.
No kernel may reach another device: no remote copies, remote signals or barrier semaphores. Data moves between devices by JAX's collectives and lax.ppermute only.
A program may use at most 128 MiB of HBM per device.

v0:
```python
import functools
import math

import jax
import jax.numpy as jnp
from jax import lax
from jax.sharding import PartitionSpec as P

HEADS = 4


LEAKY_SLOPE = 0.2
GROUP_LIMIT = 16


def passed_along(block, axis, distance):
    devices = range(lax.axis_size(axis))
    route = [((i - distance) % len(devices), i) for i in devices]
    return lax.ppermute(block, axis, route)


def add_group(step_index, running, query_tiles, key_part, value_part, edge_part, slot_list, sizes):
    numerator, denominator = running
    group_size, key_tiles, row_tiles, head_count, head_dim, score_scale, edge_scale = sizes
    tile_size = key_part.shape[1]
    feat_width = key_part.shape[2]
    in_use = slot_list >= 0
    safe_ids = jnp.where(in_use, slot_list, 0)
    row_tile = safe_ids // key_tiles
    col_tile = safe_ids % key_tiles
    query_sel = jnp.take(query_tiles, row_tile, axis=0).reshape(
        group_size, tile_size, head_count, head_dim
    )
    key_sel = jnp.take(key_part, col_tile, axis=0).reshape(
        group_size, tile_size, head_count, head_dim
    )
    value_sel = jnp.take(value_part, col_tile, axis=0).reshape(
        group_size, tile_size, head_count, head_dim
    )
    scores = (
        jnp.einsum("gqhd,gkhd->ghqk", query_sel, key_sel, preferred_element_type=jnp.float32)
        * score_scale
    )
    weights = (
        jnp.where(scores > 0, scores, LEAKY_SLOPE * scores)
        * edge_part.astype(jnp.float32)[:, None]
        * edge_scale
    )
    weights = weights * in_use[:, None, None, None].astype(jnp.float32)
    row_iota = jnp.arange(row_tiles, dtype=jnp.int32)
    one_hot = ((row_tile[:, None] == row_iota[None, :]) & in_use[:, None]).astype(jnp.float32)
    squares = jnp.sum(weights * weights, axis=3)
    denominator = denominator + jnp.einsum(
        "gr,ghq->rhq", one_hot, squares, precision=lax.Precision.HIGHEST
    )
    blended = jnp.einsum(
        "ghqk,gkhd->gqhd",
        weights.astype(jnp.bfloat16),
        value_sel,
        preferred_element_type=jnp.float32,
    )
    blended = blended.reshape(group_size, tile_size, feat_width)
    numerator = numerator + jnp.einsum(
        "gr,gqf->rqf", one_hot, blended, precision=lax.Precision.HIGHEST
    )
    return (numerator, denominator)


def on_device(queries, keys, values, tiles, edges):
    fibers = lax.axis_size("fiber")
    key_rows, feat_width = keys.shape
    stop_count = tiles.shape[2]
    capacity = tiles.shape[3]
    tile_size = edges.shape[-1]
    head_count = HEADS
    head_dim = feat_width // head_count
    row_tiles = key_rows * fibers // tile_size
    key_tiles = key_rows // tile_size
    group_size = math.gcd(capacity, GROUP_LIMIT)
    score_scale = head_dim ** (-0.5)
    edge_scale = (stop_count * fibers * key_rows / 4) ** (-0.5)
    sizes = (group_size, key_tiles, row_tiles, head_count, head_dim, score_scale, edge_scale)
    gathered = lax.all_gather(queries, "fiber", axis=0, tiled=True)
    query_tiles = gathered.reshape(row_tiles, tile_size, feat_width)
    own_edges = edges[0, 0]
    tile_lists = tiles[0, 0]
    arrivals = [(keys, values, own_edges[0])]
    for stop_index in range(1, stop_count):
        arrivals.append(passed_along((keys, values, own_edges[stop_index]), "blk", stop_index))
    running = (
        jnp.zeros((row_tiles, tile_size, feat_width), jnp.float32),
        jnp.zeros((row_tiles, head_count, tile_size), jnp.float32),
    )
    for stop_index in range(stop_count):
        key_part, value_part, edge_part = arrivals[stop_index]
        key_part = key_part.reshape(key_tiles, tile_size, feat_width)
        value_part = value_part.reshape(key_tiles, tile_size, feat_width)
        slot_list = tile_lists[stop_index]
        step_fn = functools.partial(
            add_group,
            query_tiles=query_tiles,
            key_part=key_part,
            value_part=value_part,
            edge_part=edge_part,
            slot_list=slot_list,
            sizes=sizes,
        )
        group_total = capacity // group_size
        running = lax.fori_loop(0, group_total, step_fn, running)
    numerator, denominator = running
    numerator, denominator = lax.psum((numerator, denominator), "fiber")
    position = lax.axis_index("fiber") * key_tiles
    numerator = lax.dynamic_slice_in_dim(numerator, position, key_tiles, 0)
    denominator = lax.dynamic_slice_in_dim(denominator, position, key_tiles, 0)
    spread = jnp.sqrt(1.0 + jnp.transpose(denominator, (0, 2, 1)))
    result = numerator.reshape(key_tiles, tile_size, head_count, head_dim) / spread[..., None]
    return result.reshape(key_rows, feat_width).astype(jnp.bfloat16)


def solution(mesh):
    return jax.shard_map(
        on_device,
        mesh=mesh,
        in_specs=(
            P(("blk", "fiber"), None),
            P(("blk", "fiber"), None),
            P(("blk", "fiber"), None),
            P("blk", "fiber", None, None),
            P("blk", "fiber", None, None, None, None),
        ),
        out_specs=P(("blk", "fiber"), None),
        check_vma=False,
    )
```

profile of v0, /device:TPU:0, one launch (start us, length us, event | category | flops | bytes accessed | tf_op | source)
XLA Modules:
  0.0 110.0 jit_solution(2393590291138220829)
XLA Ops:
  7.0 3.8 %collective-permute-start.7 = (bf16[256,256]{1,0:T(8,128)(2,1)}, bf16[256,256]{1,0:T(8,128)(2,1)S(1)}, u32[]{:S(2)}, u32[]{:S(2)}) collective-permute-start(bf16[256,256]{1,0:T(8,128)(2,1)} %param.10), channel_id=1, source_target_pairs={{26,0},{28,2},{30,4},{0,6},{2,8},{4,10},{6,12},{8,14},{10,16},{12,... | collective-permute-start | bytes 393224 | tf_op jit(solution)/shard_map/ppermute | solution.py:19
  10.7 1.5 %collective-permute-start.4 = (bf16[256,256]{1,0:T(8,128)(2,1)}, bf16[256,256]{1,0:T(8,128)(2,1)S(1)}, u32[]{:S(2)}, u32[]{:S(2)}) collective-permute-start(bf16[256,256]{1,0:T(8,128)(2,1)} %param.10), channel_id=1, source_target_pairs={{28,0},{30,2},{0,4},{2,6},{4,8},{6,10},{8,12},{10,14},{12,16},{14,... | collective-permute-start | bytes 393224 | tf_op jit(solution)/shard_map/ppermute | solution.py:19
  12.2 2.8 %collective-permute-start.6 = (bf16[256,256]{1,0:T(8,128)(2,1)}, bf16[256,256]{1,0:T(8,128)(2,1)S(1)}, u32[]{:S(2)}, u32[]{:S(2)}) collective-permute-start(bf16[256,256]{1,0:T(8,128)(2,1)} %param.11), channel_id=1, source_target_pairs={{26,0},{28,2},{30,4},{0,6},{2,8},{4,10},{6,12},{8,14},{10,16},{12,... | collective-permute-start | bytes 393224 | tf_op jit(solution)/shard_map/ppermute | solution.py:19
  15.0 1.3 %compare_and_fusion.1 = (pred[4]{0:T(512)(128)(4,1)}, s32[4]{0:T(128)}, s32[4]{0:T(128)S(1)}, pred[4]{0:T(512)(128)(4,1)}) fusion(s32[1,1,4,4]{3,2,1,0:T(4,128)} %param.12), kind=kLoop, calls=%fused_computation.105 | loop fusion | flops 76 | bytes 56 | tf_op jit(solution)/shard_map/while/body/eval_jaxpr/jit(_take)/and | solution.py:37
  16.3 0.6 broadcast_select_fusion.12
  16.9 0.6 compare_and_fusion
  17.5 0.6 compare_and_fusion.2
  18.1 0.5 copy-done.20
  18.7 1.5 %gather_fusion.2 = bf16[4,128,256]{2,1,0:T(8,128)(2,1)S(1)} fusion(bf16[2,128,256]{2,1,0:T(8,128)(2,1)} %bitcast.161, s32[1024]{0:T(1024)S(1)} %pad_clamp_fusion.7), kind=kCustom, calls=%fused_computation.2.clone | custom fusion | bytes 524304 | tf_op jit(solution)/shard_map/while/body/eval_jaxpr/jit(_take)/gather | solution.py:34
  20.3 0.6 gather_fusion
  20.9 0.8 copy.57
  22.0 0.7 copy-done.13
  22.7 5.6 %all_gather.3 = bf16[512,256]{1,0:T(8,128)(2,1)S(1)} all-gather(bf16[256,256]{1,0:T(8,128)(2,1)S(1)} %copy-done.13), channel_id=1, replica_groups=mesh['blk'=16,'fiber'=2] {'fiber'}, dimensions={0}, use_global_device_ids=true | all-gather | bytes 393216 | tf_op jit(solution)/shard_map/all_gather | solution.py:83
  28.3 0.6 gather_fusion.10
  28.9 0.6 gather_fusion.7
  29.5 0.6 gather_fusion.4
  30.0 0.6 gather_fusion.1
  30.9 0.8 copy-done.9
  31.6 0.7 slice_bitcast_fusion
  33.3 0.6 copy-done.11
  34.6 0.6 copy-done.31
  35.3 0.7 copy-done.33
  36.1 0.6 copy-done.32
  36.8 0.6 fusion.53
  37.4 0.7 fusion.24
  38.1 0.6 copy-done.35
  38.7 1.6 %collective-permute-start.3 = (bf16[256,256]{1,0:T(8,128)(2,1)S(1)}, bf16[256,256]{1,0:T(8,128)(2,1)S(1)}, u32[]{:S(2)}, u32[]{:S(2)}) collective-permute-start(bf16[256,256]{1,0:T(8,128)(2,1)S(1)} %copy-done.8), channel_id=1, source_target_pairs={{28,0},{30,2},{0,4},{2,6},{4,8},{6,10},{8,12},{10,14},{12,16},{14,... | collective-permute-start | bytes 393224 | tf_op jit(solution)/shard_map/ppermute | solution.py:19
  40.7 0.8 copy.64
  41.5 0.6 copy-done.34
  42.1 0.6 gather_fusion.5
  42.7 0.6 gather_fusion.3
  43.3 1.0 collective-permute-start.2
  44.3 0.6 gather_fusion.11
  44.9 1.1 collective-permute-start.5
  46.0 0.6 gather_fusion.9
  46.6 0.6 gather_fusion.8
  47.2 0.6 gather_fusion.6
  47.8 0.7 copy-done.30
  48.7 0.7 copy-done.37
  49.4 1.0 broadcast_select_fusion.5
  51.0 0.8 copy-done.7
  51.7 0.8 copy.69
  52.7 0.9 copy.71
  53.6 0.8 copy.65
  54.5 0.8 copy.63
  55.3 1.0 copy.78
  57.3 1.5 %fusion.14 = (u8[4,128,128]{1,2,0:T(8,128)(4,1)S(1)}, f32[4,4,128,128]{2,3,1,0:T(8,128)S(1)}) fusion(bf16[4,128,4,64]{1,3,2,0:T(8,128)(2,1)} %bitcast.152, bf16[4,128,4,64]{1,3,2,0:T(8,128)(2,1)} %bitcast.156), kind=kOutput, calls=%fused_computation.47 | convolution fusion | flops 35061760 | bytes 1638400 | tf_op jit(solution)/shard_map/while/body/eval_jaxpr/gqhd,gkhd->ghqk/dot_general | solution.py:41
  59.1 1.0 copy.66
  60.9 1.0 copy.68
  61.9 1.4 %fusion.15 = (u8[4,128,128]{1,2,0:T(8,128)(4,1)S(1)}, f32[4,4,128,128]{2,3,1,0:T(8,128)S(1)}) fusion(bf16[4,128,4,64]{1,3,2,0:T(8,128)(2,1)S(1)} %bitcast.151, bf16[4,128,4,64]{1,3,2,0:T(8,128)(2,1)} %bitcast.154), kind=kOutput, calls=%fused_computation.48 | convolution fusion | flops 35061760 | bytes 1638400 | tf_op jit(solution)/shard_map/while/body/eval_jaxpr/gqhd,gkhd->ghqk/dot_general | solution.py:41
  63.7 1.0 copy.72
  64.7 0.7 copy-done.25
  65.7 0.6 copy-done.10
  67.0 0.8 copy-done
  67.8 0.6 convolution_add_fusion.2
  68.5 0.6 copy-done.19
  69.1 0.6 convolution_add_fusion.1
  69.8 0.6 copy-done.17
  70.4 1.4 %convolution_add_fusion = f32[4,128,256]{2,0,1:T(4,128)} fusion(f32[4,128,256]{2,0,1:T(4,128)S(1)} %convolution_add_fusion.1, f32[4,128,256]{2,0,1:T(4,128)S(1)} %copy.80, s32[4]{0:T(128)S(1)} %copy-done.17, pred[4]{0:T(512)(128)(4,1)S(1)} %copy-done.22), kind=kOutput, calls=%fused_computation.12 | convolution fusion | flops 6422560 | bytes 1572884 | tf_op jit(solution)/shard_map/while/body/eval_jaxpr/gr,gqf->rqf/dot_general | solution.py:63
  71.9 0.7 copy-done.14
  73.0 5.0 %psum.15 = f32[4,4,128]{2,0,1:T(4,128)S(1)} all-reduce(f32[4,4,128]{2,0,1:T(4,128)S(1)} %convolution_add_fusion.3), channel_id=1, replica_groups=mesh['blk'=16,'fiber'=2] {'fiber'}, use_global_device_ids=true, to_apply=%region_5.8 | all-reduce | flops 2048 | bytes 16384 | tf_op jit(solution)/shard_map/psum | solution.py:111
  78.2 23.1 %all-reduce.2.cloned.1.call-done = f32[4,128,256]{2,0,1:T(4,128)} async-done(((f32[4,128,256]{2,0,1:T(4,128)}), f32[4,128,256]{2,0,1:T(4,128)}) %all-reduce.2.cloned.1.call-update) | async-done | bytes 524304 | tf_op jit(solution)/shard_map/psum | solution.py:111
  101.3 1.2 %constant_dynamic-slice_fusion = f32[2,128,256]{2,0,1:T(2,128)S(1)} fusion(f32[4,128,256]{2,0,1:T(4,128)} %all-reduce.2.cloned.1.call-done, s32[]{:T(128)S(6)} %select_n.143), kind=kLoop, calls=%fused_computation.140 | loop fusion | bytes 524292 | tf_op jit(solution)/shard_map/dynamic_slice | solution.py:113
  102.5 0.7 fusion.12
  (118 shorter events, 8.7 us)
Async XLA Ops:
  6.5 9.7 %copy-start.15 = (s32[1,1,4,4]{3,2,1,0:T(4,128)S(1)}, s32[1,1,4,4]{3,2,1,0:T(4,128)}, u32[]{:S(2)}) copy-start(s32[1,1,4,4]{3,2,1,0:T(4,128)} %param.12) | copy-start | bytes 196
  6.5 94.7 %all-reduce.2.cloned.1.call-start = ((), (), s32[]{:S(2)}) async-start(), calls=%async_computation | async-start | bytes 1048576 | tf_op jit(solution)/shard_map/psum | solution.py:111
  6.5 32.1 %collective-permute-start.1 = (bf16[256,256]{1,0:T(8,128)(2,1)}, bf16[256,256]{1,0:T(8,128)(2,1)S(1)}, u32[]{:S(2)}, u32[]{:S(2)}) collective-permute-start(bf16[256,256]{1,0:T(8,128)(2,1)} %param.10), channel_id=1, source_target_pairs={{30,0},{0,2},{2,4},{4,6},{6,8},{8,10},{10,12},{12,14},{14,16},{16,... | collective-permute-start | bytes 393224 | tf_op jit(solution)/shard_map/ppermute | solution.py:19
  7.0 36.3 %collective-permute-start.7 = (bf16[256,256]{1,0:T(8,128)(2,1)}, bf16[256,256]{1,0:T(8,128)(2,1)S(1)}, u32[]{:S(2)}, u32[]{:S(2)}) collective-permute-start(bf16[256,256]{1,0:T(8,128)(2,1)} %param.10), channel_id=1, source_target_pairs={{26,0},{28,2},{30,4},{0,6},{2,8},{4,10},{6,12},{8,14},{10,16},{12,... | collective-permute-start | bytes 393224 | tf_op jit(solution)/shard_map/ppermute | solution.py:19
  10.7 35.8 %collective-permute-start.4 = (bf16[256,256]{1,0:T(8,128)(2,1)}, bf16[256,256]{1,0:T(8,128)(2,1)S(1)}, u32[]{:S(2)}, u32[]{:S(2)}) collective-permute-start(bf16[256,256]{1,0:T(8,128)(2,1)} %param.10), channel_id=1, source_target_pairs={{28,0},{30,2},{0,4},{2,6},{4,8},{6,10},{8,12},{10,14},{12,16},{14,... | collective-permute-start | bytes 393224 | tf_op jit(solution)/shard_map/ppermute | solution.py:19
  12.2 30.4 %collective-permute-start = (bf16[256,256]{1,0:T(8,128)(2,1)}, bf16[256,256]{1,0:T(8,128)(2,1)S(1)}, u32[]{:S(2)}, u32[]{:S(2)}) collective-permute-start(bf16[256,256]{1,0:T(8,128)(2,1)} %param.11), channel_id=1, source_target_pairs={{30,0},{0,2},{2,4},{4,6},{6,8},{8,10},{10,12},{12,14},{14,16},{16,... | collective-permute-start | bytes 393224 | tf_op jit(solution)/shard_map/ppermute | solution.py:19
  12.2 32.7 %collective-permute-start.6 = (bf16[256,256]{1,0:T(8,128)(2,1)}, bf16[256,256]{1,0:T(8,128)(2,1)S(1)}, u32[]{:S(2)}, u32[]{:S(2)}) collective-permute-start(bf16[256,256]{1,0:T(8,128)(2,1)} %param.11), channel_id=1, source_target_pairs={{26,0},{28,2},{30,4},{0,6},{2,8},{4,10},{6,12},{8,14},{10,16},{12,... | collective-permute-start | bytes 393224 | tf_op jit(solution)/shard_map/ppermute | solution.py:19
  16.9 16.1 %copy-start.28 = (f32[4]{0:T(128)}, f32[4]{0:T(128)S(1)}, u32[]{:S(2)}) copy-start(f32[4]{0:T(128)S(1)} %get-tuple-element.130) | copy-start | bytes 52
  16.9 43.4 %copy-start.26 = (f32[4]{0:T(128)}, f32[4]{0:T(128)S(1)}, u32[]{:S(2)}) copy-start(f32[4]{0:T(128)S(1)} %get-tuple-element.128) | copy-start | bytes 52
  17.5 1.2 %copy-start.16 = (s32[4]{0:T(128)}, s32[4]{0:T(128)S(1)}, u32[]{:S(2)}) copy-start(s32[4]{0:T(128)S(1)} %get-tuple-element.81) | copy-start | bytes 52
  18.1 0.5 copy-start.20
  18.1 0.6 copy-start.18
  18.7 1.5 %copy-start.8 = (bf16[256,256]{1,0:T(8,128)(2,1)S(1)}, bf16[256,256]{1,0:T(8,128)(2,1)}, u32[]{:S(2)}) copy-start(bf16[256,256]{1,0:T(8,128)(2,1)} %param.11) | copy-start | bytes 393220
  21.8 0.9 copy-start.13
  30.6 1.0 copy-start.9
  32.9 1.0 copy-start.11
  33.3 0.6 copy-start.29
  34.6 0.6 copy-start.31
  35.3 0.7 copy-start.33
  36.1 0.6 copy-start.32
  38.1 0.6 copy-start.35
  38.7 1.6 %copy-start.36 = (s32[4]{0:T(128)S(1)}, s32[4]{0:T(128)}, u32[]{:S(2)}) copy-start(s32[4]{0:T(128)} %get-tuple-element.133) | copy-start | bytes 52
  38.7 8.5 %collective-permute-start.3 = (bf16[256,256]{1,0:T(8,128)(2,1)S(1)}, bf16[256,256]{1,0:T(8,128)(2,1)S(1)}, u32[]{:S(2)}, u32[]{:S(2)}) collective-permute-start(bf16[256,256]{1,0:T(8,128)(2,1)S(1)} %copy-done.8), channel_id=1, source_target_pairs={{28,0},{30,2},{0,4},{2,6},{4,8},{6,10},{8,12},{10,14},{12,16},{14,... | collective-permute-start | bytes 393224 | tf_op jit(solution)/shard_map/ppermute | solution.py:19
  41.5 0.6 copy-start.34
  42.7 12.6 %collective-permute-start.8 = (bf16[4,128,128]{2,1,0:T(8,128)(2,1)}, bf16[4,128,128]{2,1,0:T(8,128)(2,1)}, u32[]{:S(2)}, u32[]{:S(2)}) collective-permute-start(bf16[4,128,128]{2,1,0:T(8,128)(2,1)} %get-tuple-element.113), channel_id=1, source_target_pairs={{26,0},{28,2},{30,4},{0,6},{2,8},{4,10},{6,12},{8,14},{10,16},{12,... | collective-permute-start | bytes 393224 | tf_op jit(solution)/shard_map/ppermute | solution.py:19
  43.3 15.8 %collective-permute-start.2 = (bf16[4,128,128]{2,1,0:T(8,128)(2,1)}, bf16[4,128,128]{2,1,0:T(8,128)(2,1)}, u32[]{:S(2)}, u32[]{:S(2)}) collective-permute-start(bf16[4,128,128]{2,1,0:T(8,128)(2,1)} %get-tuple-element.114), channel_id=1, source_target_pairs={{30,0},{0,2},{2,4},{4,6},{6,8},{8,10},{10,12},{12,14},{14,16},{16,... | collective-permute-start | bytes 393224 | tf_op jit(solution)/shard_map/ppermute | solution.py:19
  44.9 18.8 %collective-permute-start.5 = (bf16[4,128,128]{2,1,0:T(8,128)(2,1)}, bf16[4,128,128]{2,1,0:T(8,128)(2,1)}, u32[]{:S(2)}, u32[]{:S(2)}) collective-permute-start(bf16[4,128,128]{2,1,0:T(8,128)(2,1)} %get-tuple-element.116), channel_id=1, source_target_pairs={{28,0},{30,2},{0,4},{2,6},{4,8},{6,10},{8,12},{10,14},{12,16},{14,... | collective-permute-start | bytes 393224 | tf_op jit(solution)/shard_map/ppermute | solution.py:19
  47.7 0.7 copy-start.30
  48.7 0.7 copy-start.37
  48.7 0.7 copy-start.38
  50.8 1.0 copy-start.7
  51.7 0.9 copy-start.6
  52.7 0.9 copy-start.5
  56.3 0.7 copy-start.1
  57.3 1.5 %copy-start.2 = (f32[4,128,128]{1,2,0:T(8,128)S(1)}, f32[4,128,128]{1,2,0:T(8,128)}, u32[]{:S(2)}) copy-start(f32[4,128,128]{1,2,0:T(8,128)} %copy-done.1) | copy-start | bytes 786436
  59.1 1.1 copy-start.12
  60.2 0.7 copy-start.3
  61.9 1.4 %copy-start.4 = (f32[4,128,128]{1,2,0:T(8,128)S(1)}, f32[4,128,128]{1,2,0:T(8,128)}, u32[]{:S(2)}) copy-start(f32[4,128,128]{1,2,0:T(8,128)} %copy-done.3) | copy-start | bytes 786436
  61.9 1.4 %copy-start.27 = (f32[4]{0:T(128)S(1)}, f32[4]{0:T(128)}, u32[]{:S(2)}) copy-start(f32[4]{0:T(128)} %copy-done.26) | copy-start | bytes 52
  64.7 0.7 copy-start.25
  65.4 0.9 copy-start.10
  66.8 1.1 copy-start
  67.0 0.8 copy-start.21
  67.0 0.8 copy-start.24
  68.4 0.6 copy-start.19
  68.4 0.7 copy-start.23
  69.7 0.7 copy-start.17
  69.8 0.7 copy-start.22
  71.9 0.7 copy-start.14
Sparse Core Ops, SparseCore 0:
  72.0 29.2 all-reduce.1
where the time goes:
time: 111 us; the launch traced here: 110 us
  local copies, waits for them, and re-layouts  32.5 us (29%)
  waiting for transfers between devices  23.1 us (21%)
  between operations  14.1 us (13%)
  starting transfers between devices  12.2 us (11%)
  blocking collectives  10.6 us (10%)
  matrix products  9.86 us (9%)
  other arithmetic  7.58 us (7%)
    psum x1, waiting for transfers between devices, on_device(): numerator, denominator = lax.psum((numerator, denominator), 'fiber')  23.1 us
    unnamed x79, local copies, waits for them, and re-layouts  12.5 us
    ppermute x9, starting transfers between devices, passed_along(): return lax.ppermute(block, axis, route)  12.2 us
    all_gather x1, blocking collectives, on_device(): gathered = lax.all_gather(queries, 'fiber', axis=0, tiled=True)  5.63 us
    psum x1, blocking collectives, on_device(): numerator, denominator = lax.psum((numerator, denominator), 'fiber')  4.99 us
    dot_general x4, matrix products, add_group(): jnp.einsum('gqhd,gkhd->ghqk', query_sel, key_sel, preferred_element_type=...  3.69 us
    dot_general x4, matrix products, add_group(): jnp.einsum('gr,gqf->rqf', one_hot, blended, precision=lax.Precision.HIGHEST)  3.25 us
    gather x4, local copies, waits for them, and re-layouts, add_group(): jnp.take(key_part, col_tile, axis=0)  3.19 us
  transfers between devices with their start and end apart: 10, of which 1 were waited for; matrix products, arithmetic and copies ran while one was open for 28% of the time, Pallas kernels for 0%

commit v1 on v0

v1 whole, which is shorter than its diff:
```python
import functools
import math

import jax
import jax.numpy as jnp
from jax import lax
from jax.experimental import pallas as pl
from jax.experimental.pallas import tpu as pltpu
from jax.sharding import PartitionSpec as P

HEADS = 4
LEAKY_SLOPE = 0.2
CORES = 2
UNROLL = 4
EXTRA_ROWS = 16
LANES = 128
VMEM_BYTES = 24 * 2**20


def moved(block, axis, distance):
    count = lax.axis_size(axis)
    return lax.ppermute(block, axis, [((i - distance) % count, i) for i in range(count)])


def routed(block, source_of):
    count = lax.axis_size("blk")
    return lax.ppermute(block, "blk", [(source_of(i) % count, i) for i in range(count)])


def head_masked(block, head_count):
    head_dim = block.shape[1] // head_count
    head_of = lax.broadcasted_iota(jnp.int32, block.shape, 1) // head_dim
    return jnp.concatenate(
        [jnp.where(head_of == h, block, jnp.zeros_like(block)) for h in range(head_count)], axis=0
    )


def attend_kernel(tiles_ref, *refs, stop_ids, fibers, key_tiles, tile, head_count, scale):
    stops = len(stop_ids)
    queries = refs[:fibers]
    blocks = refs[fibers : fibers + 3 * stops]
    num_ref, den_ref = refs[fibers + 3 * stops : fibers + 3 * stops + 2]
    payload_ref = refs[fibers + 3 * stops + 2]
    query_ref, sums_ref, squares_ref = refs[fibers + 3 * stops + 3 :]
    rows, feats = queries[0].shape
    capacity = tiles_ref.shape[-1]
    group = math.gcd(capacity, UNROLL)
    fiber = lax.axis_index("fiber")
    core = lax.rem(lax.axis_index("blk"), CORES)
    for r in range(fibers):
        query_ref[r * rows : (r + 1) * rows, :] = queries[r][...]
    sums_ref[...] = jnp.zeros_like(sums_ref)
    squares_ref[...] = jnp.zeros_like(squares_ref)
    for n, stop_of in enumerate(stop_ids):
        key_ref, value_ref, edge_ref = blocks[3 * n : 3 * n + 3]
        stop = stop_of(core)
        keys = [head_masked(key_ref[c * tile : (c + 1) * tile, :], head_count) for c in range(key_tiles)]
        values = [head_masked(value_ref[c * tile : (c + 1) * tile, :], head_count) for c in range(key_tiles)]

        def one_group(g, carry, keys=keys, values=values, edge_ref=edge_ref, stop=stop):
            for k in range(group):
                slot = g * group + k
                listed = tiles_ref[0, 0, stop, slot]
                used = listed >= 0
                number = jnp.maximum(listed, 0)
                row_tile = lax.div(number, key_tiles)
                col_tile = lax.rem(number, key_tiles)
                part = lax.rem(lax.div(row_tile, key_tiles) - fiber + fibers, fibers)
                at = pl.multiple_of((part * key_tiles + lax.rem(row_tile, key_tiles)) * tile, tile)
                key_stack, value_stack = keys[0], values[0]
                for c in range(1, key_tiles):
                    key_stack = jnp.where(col_tile == c, keys[c], key_stack)
                    value_stack = jnp.where(col_tile == c, values[c], value_stack)
                scores = lax.dot_general(
                    query_ref[pl.ds(at, tile), :],
                    key_stack,
                    (((1,), (1,)), ((), ())),
                    preferred_element_type=jnp.float32,
                )
                edge = jnp.where(used, edge_ref[slot].astype(jnp.float32) * scale, 0.0)
                weights = jnp.maximum(scores, LEAKY_SLOPE * scores) * jnp.concatenate([edge] * head_count, axis=1)
                squares_ref[pl.ds(at, tile), :] += weights * weights
                sums_ref[pl.ds(at, tile), :] += jnp.dot(
                    weights.astype(jnp.bfloat16), value_stack, preferred_element_type=jnp.float32
                )
            return carry

        if capacity == group:
            one_group(0, 0)
        else:
            lax.fori_loop(0, capacity // group, one_group, 0)

    lane = lax.broadcasted_iota(jnp.int32, (tile, LANES), 1)

    def totals(at):
        den = jnp.zeros((tile, LANES), jnp.float32)
        for h in range(head_count):
            total = jnp.sum(squares_ref[at : at + tile, h * tile : (h + 1) * tile], axis=1, keepdims=True)
            den = jnp.where(lane == h, total, den)
        return den

    num_ref[...] = sums_ref[:rows, :]
    for t in range(key_tiles):
        den_ref[t * tile : (t + 1) * tile, :] = totals(t * tile)
    for r in range(1, fibers):
        payload_ref[r - 1, :rows, :] = sums_ref[r * rows : (r + 1) * rows, :].astype(jnp.bfloat16)
        for t in range(key_tiles):
            den = totals(r * rows + t * tile)
            high = den.astype(jnp.bfloat16)
            rest = (den - high.astype(jnp.float32)).astype(jnp.bfloat16)
            half = EXTRA_ROWS // 2
            both = jnp.concatenate(
                [high.astype(jnp.float32).T[:half], rest.astype(jnp.float32).T[:half]], axis=0
            )
            payload_ref[r - 1, rows : rows + EXTRA_ROWS, t * tile : (t + 1) * tile] = both.astype(jnp.bfloat16)


def finish_kernel(num_ref, den_ref, *refs, key_tiles, tile, head_count):
    *payloads, out_ref = refs
    rows, feats = num_ref.shape
    head_dim = feats // head_count
    half = EXTRA_ROWS // 2
    head_of = lax.broadcasted_iota(jnp.int32, (tile, feats), 1) // head_dim
    for t in range(key_tiles):
        here = slice(t * tile, (t + 1) * tile)
        num = num_ref[here, :]
        den = den_ref[here, :]
        for payload in payloads:
            num = num + payload[here, :].astype(jnp.float32)
            both = payload[rows : rows + EXTRA_ROWS, here].astype(jnp.float32)
            total = both[:half] + both[half:]
            padded = jnp.concatenate([total, jnp.zeros((LANES - half, tile), jnp.float32)], axis=0)
            den = den + padded.T
        spread = lax.rsqrt(1.0 + den)
        factor = jnp.broadcast_to(spread[:, 0:1], (tile, feats))
        for h in range(1, head_count):
            factor = jnp.where(head_of == h, spread[:, h : h + 1], factor)
        out_ref[here, :] = (num * factor).astype(jnp.bfloat16)


def on_device(queries, keys, values, tiles, edges):
    fibers = lax.axis_size("fiber")
    rows, feats = keys.shape
    stops, capacity, tile = tiles.shape[2], tiles.shape[3], edges.shape[-1]
    key_tiles = rows // tile
    head_dim = feats // HEADS
    scale = head_dim ** (-0.5) * (stops * fibers * rows / 4) ** (-0.5)
    core = lax.rem(lax.axis_index("blk"), CORES)
    own_edges = edges[0, 0]

    def edges_of(stop):
        return lax.dynamic_index_in_dim(own_edges, stop, 0, keepdims=False)

    blocks = [(keys, values, edges)]
    stop_ids = [lambda core: 0]
    for m in range(1, stops // 2):
        shift = CORES * m
        far_keys, far_values = moved((keys, values), "blk", shift)
        far_edges = moved(own_edges[shift], "blk", shift)
        cross_edges = edges_of(jnp.where(core == 1, shift - 1, shift + 1))
        cross_edges = routed(cross_edges, lambda i, shift=shift: (i - shift) ^ 1)
        near_keys, near_values = routed((far_keys, far_values), lambda i: i ^ 1)
        blocks.append((far_keys, far_values, far_edges))
        stop_ids.append(lambda core, shift=shift: shift)
        blocks.append((near_keys, near_values, cross_edges))
        stop_ids.append(lambda core, shift=shift: jnp.where(core == 0, shift - 1, shift + 1))
    last_edges = edges_of(jnp.where(core == 1, stops - 1, 1))
    blocks.append(
        routed((keys, values, last_edges), lambda i: i - 1 if i % CORES else i - stops + 1)
    )
    stop_ids.append(lambda core: jnp.where(core == 0, stops - 1, 1))
    all_queries = [queries] + [moved(queries, "fiber", -r) for r in range(1, fibers)]

    whole = pl.BlockSpec(memory_space=pltpu.VMEM)
    own_list = pl.BlockSpec((None, None, None, capacity, tile, tile), lambda i: (0, 0, 0, 0, 0, 0))
    num, den, payload = pl.pallas_call(
        functools.partial(
            attend_kernel,
            stop_ids=stop_ids,
            fibers=fibers,
            key_tiles=key_tiles,
            tile=tile,
            head_count=HEADS,
            scale=scale,
        ),
        grid=(1,),
        in_specs=[pl.BlockSpec(memory_space=pltpu.SMEM)]
        + [whole] * fibers
        + [whole, whole, own_list]
        + [whole] * (3 * (stops - 1)),
        out_specs=[whole] * 3,
        out_shape=[
            jax.ShapeDtypeStruct((rows, feats), jnp.float32),
            jax.ShapeDtypeStruct((rows, LANES), jnp.float32),
            jax.ShapeDtypeStruct((max(fibers - 1, 1), rows + EXTRA_ROWS, feats), jnp.bfloat16),
        ],
        scratch_shapes=[
            pltpu.VMEM((fibers * rows, feats), jnp.bfloat16),
            pltpu.VMEM((fibers * rows, feats), jnp.float32),
            pltpu.VMEM((fibers * rows, HEADS * tile), jnp.float32),
        ],
        compiler_params=pltpu.CompilerParams(vmem_limit_bytes=VMEM_BYTES),
    )(tiles, *all_queries, *[part for block in blocks for part in block])
    arrived = [moved(payload[r - 1], "fiber", r) for r in range(1, fibers)]
    return pl.pallas_call(
        functools.partial(finish_kernel, key_tiles=key_tiles, tile=tile, head_count=HEADS),
        in_specs=[whole] * (2 + len(arrived)),
        out_specs=whole,
        out_shape=jax.ShapeDtypeStruct((rows, feats), jnp.bfloat16),
        compiler_params=pltpu.CompilerParams(vmem_limit_bytes=VMEM_BYTES),
    )(num, den, *arrived)


def solution(mesh):
    return jax.shard_map(
        on_device,
        mesh=mesh,
        in_specs=(
            P(("blk", "fiber"), None),
            P(("blk", "fiber"), None),
            P(("blk", "fiber"), None),
            P("blk", "fiber", None, None),
            P("blk", "fiber", None, None, None, None),
        ),
        out_specs=P(("blk", "fiber"), None),
        check_vma=False,
    )
```

time: 111 us -> 36.2 us (0.33)
  local copies, waits for them, and re-layouts: 32.5 us -> 2.01 us
  between operations: 14.1 us -> 0.06 us
  blocking collectives: 10.6 us -> 0 us
  matrix products: 9.86 us -> 0 us
  other arithmetic: 7.58 us -> 0 us
  waiting for transfers between devices: 23.1 us -> 16.2 us
  Pallas kernels: 0 us -> 5.32 us
    psum x1 -> x0, waiting for transfers between devices: 23.1 us -> none  [on_device(): numerator, denominator = lax.psum((numerator, denominator), 'fiber')]
    ppermute x9 -> x11, waiting for transfers between devices: 0.02 us -> 16.2 us  [the longest x5 10.2 us: moved(): lax.ppermute(block, axis, [((i - distance) % count, i) for i in range(cou...]
    unnamed x79 -> x10, local copies, waits for them, and re-layouts: 12.5 us -> 0.91 us
    dot_general x16 -> x0, matrix products: 9.86 us -> none  [the longest x4 3.69 us: add_group(): jnp.einsum('gqhd,gkhd->ghqk', query_sel, key_sel, preferred_element_type=...]
    gather x12 -> x0, local copies, waits for them, and re-layouts: 7.7 us -> none  [the longest x4 3.19 us: add_group(): jnp.take(key_part, col_tile, axis=0)]
    select_n x12 -> x0, local copies, waits for them, and re-layouts: 6.05 us -> none  [the longest x4 2.67 us: add_group(): jnp.take(value_part, col_tile, axis=0)]
    all_gather x1 -> x0, blocking collectives: 5.63 us -> none  [on_device(): gathered = lax.all_gather(queries, 'fiber', axis=0, tiled=True)]
    pallas_call x0 -> x2, Pallas kernels: none -> 5.32 us  [the longest x1 4.36 us: on_device(): pl.pallas_call(functools.partial(attend_kernel, stop_ids=stop_ids, fibers...]
  transfers between devices with their start and end apart: 10 -> 11, of which waited for: 1 -> 5; matrix products, arithmetic and copies ran while one was open for 28% -> 3% of each run, Pallas kernels for 0% -> 0%
where the time goes in v1:
time: 36.2 us; the launch traced here: 36 us
  waiting for transfers between devices  16.2 us (45%)
  starting transfers between devices  12.4 us (34%)
  Pallas kernels  5.32 us (15%)
  local copies, waits for them, and re-layouts  2.01 us (6%)
    ppermute x5, waiting for transfers between devices, moved(): lax.ppermute(block, axis, [((i - distance) % count, i) for i in range(cou...  10.2 us
    ppermute x5, starting transfers between devices, moved(): lax.ppermute(block, axis, [((i - distance) % count, i) for i in range(cou...  7.67 us
    ppermute x6, waiting for transfers between devices, routed(): lax.ppermute(block, 'blk', [(source_of(i) % count, i) for i in range(coun...  6 us
    ppermute x6, starting transfers between devices, routed(): lax.ppermute(block, 'blk', [(source_of(i) % count, i) for i in range(coun...  4.71 us
    pallas_call x1, Pallas kernels, on_device(): pl.pallas_call(functools.partial(attend_kernel, stop_ids=stop_ids, fibers...  4.36 us
    squeeze x1, local copies, waits for them, and re-layouts, edges_of(): return lax.dynamic_index_in_dim(own_edges, stop, 0, keepdims=False)  1.1 us
    pallas_call x1, Pallas kernels, on_device(): pl.pallas_call(functools.partial(finish_kernel, key_tiles=key_tiles, tile...  0.96 us
    unnamed x10, local copies, waits for them, and re-layouts  0.91 us
  transfers between devices with their start and end apart: 11, of which 5 were waited for; matrix products, arithmetic and copies ran while one was open for 3% of the time, Pallas kernels for 0%

profile of v1, /device:TPU:0, one launch (start us, length us, event | category | flops | bytes accessed | tf_op | source)
XLA Modules:
  0.0 36.0 jit_solution(15898017333431226921)
XLA Ops:
  0.0 0.0 copy-start
  0.0 2.9 %collective-permute-start.1 = (bf16[256,256]{1,0:T(8,128)(2,1)}, bf16[256,256]{1,0:T(8,128)(2,1)S(1)}, u32[]{:S(2)}, u32[]{:S(2)}) collective-permute-start(bf16[256,256]{1,0:T(8,128)(2,1)} %refs_2_.1), channel_id=1, source_target_pairs={{28,0},{30,2},{0,4},{2,6},{4,8},{6,10},{8,12},{10,14},{12,16},{14,... | collective-permute-start | bytes 393224 | tf_op jit(solution)/shard_map/ppermute | solution.py:22
  2.9 0.0 collective-permute-start.7
  2.9 1.5 %collective-permute-start.2 = (bf16[256,256]{1,0:T(8,128)(2,1)}, bf16[256,256]{1,0:T(8,128)(2,1)S(1)}, u32[]{:S(2)}, u32[]{:S(2)}) collective-permute-start(bf16[256,256]{1,0:T(8,128)(2,1)} %refs_3_.1), channel_id=1, source_target_pairs={{28,0},{30,2},{0,4},{2,6},{4,8},{6,10},{8,12},{10,14},{12,16},{14,... | collective-permute-start | bytes 393224 | tf_op jit(solution)/shard_map/ppermute | solution.py:22
  4.5 1.4 %collective-permute-start.8 = (bf16[256,256]{1,0:T(8,128)(2,1)}, bf16[256,256]{1,0:T(8,128)(2,1)S(1)}, u32[]{:S(2)}, u32[]{:S(2)}) collective-permute-start(bf16[256,256]{1,0:T(8,128)(2,1)} %refs_3_.1), channel_id=1, source_target_pairs={{26,0},{0,2},{30,4},{4,6},{2,8},{8,10},{6,12},{12,14},{10,16},{16,... | collective-permute-start | bytes 393224 | tf_op jit(solution)/shard_map/ppermute | solution.py:27
  5.9 1.5 %collective-permute-start = (bf16[256,256]{1,0:T(8,128)(2,1)}, bf16[256,256]{1,0:T(8,128)(2,1)S(1)}, u32[]{:S(2)}, u32[]{:S(2)}) collective-permute-start(bf16[256,256]{1,0:T(8,128)(2,1)} %refs_0_.1), channel_id=1, source_target_pairs={{1,0},{0,1},{3,2},{2,3},{5,4},{4,5},{7,6},{6,7},{9,8},{8,9},{11,10... | collective-permute-start | bytes 393224 | tf_op jit(solution)/shard_map/ppermute | solution.py:22
  7.4 0.0 copy-start.1
  7.4 0.0 copy-start.2
  7.4 1.1 %dynamic-slice_bitcast_fusion = (bf16[4,128,128]{2,1,0:T(8,128)(2,1)S(1)}, bf16[4,128,128]{2,1,0:T(8,128)(2,1)S(1)}, bf16[4,128,128]{2,1,0:T(8,128)(2,1)S(1)}) fusion(bf16[1,1,4,4,128,128]{5,4,3,2,1,0:T(8,128)(2,1)} %refs_4_.1, s32[]{:T(128)S(6)} %select_n.11, s32[]{:T(128)S(6)} %select_n.10), kind=kLoop, calls=%fused_computation | loop fusion | bytes 786440 | tf_op jit(solution)/shard_map/jit(dynamic_index_in_dim)/squeeze | solution.py:152
  8.5 3.3 %collective-permute-done.refs_1_ = bf16[256,256]{1,0:T(8,128)(2,1)S(1)} collective-permute-done((bf16[256,256]{1,0:T(8,128)(2,1)}, bf16[256,256]{1,0:T(8,128)(2,1)S(1)}, u32[]{:S(2)}, u32[]{:S(2)}) %collective-permute-start) | collective-permute-done | bytes 131104 | tf_op jit(solution)/shard_map/ppermute | solution.py:22
  11.8 0.0 copy-start.4
  11.8 0.0 collective-permute-start.9
  11.8 0.0 collective-permute-done.1.refs_5_
  11.8 2.8 %collective-permute-start.6 = (bf16[4,128,128]{2,1,0:T(8,128)(2,1)S(1)}, bf16[4,128,128]{2,1,0:T(8,128)(2,1)S(1)}, u32[]{:S(2)}, u32[]{:S(2)}) collective-permute-start(bf16[4,128,128]{2,1,0:T(8,128)(2,1)S(1)} %get-tuple-element.12), channel_id=1, source_target_pairs={{30,0},{28,2},{2,4},{0,6},{6,8},{4,10},{10,12},{8,14},{14,16},{12,... | collective-permute-start | bytes 393224 | tf_op jit(solution)/shard_map/ppermute | solution.py:27
  14.6 0.0 collective-permute-done.7.refs_11_
  14.6 0.1 collective-permute-start.3
  14.7 0.0 collective-permute-done.2.refs_6_
  14.7 0.1 collective-permute-start.4
  14.8 0.0 collective-permute-done.8.refs_12_
  14.8 0.5 %collective-permute-start.5 = (bf16[256,256]{1,0:T(8,128)(2,1)S(1)}, bf16[256,256]{1,0:T(8,128)(2,1)S(1)}, u32[]{:S(2)}, u32[]{:S(2)}) collective-permute-start(bf16[256,256]{1,0:T(8,128)(2,1)S(1)} %collective-permute-done.2.refs_6_), channel_id=1, source_target_pairs={{2,0},{0,2},{6,4},{4,6},{10,8},{8,10},{14,12},{12,14},{18,16},{16,... | collective-permute-start | bytes 393224 | tf_op jit(solution)/shard_map/ppermute | solution.py:27
  15.2 2.8 %collective-permute-done.9.refs_13_ = bf16[4,128,128]{2,1,0:T(8,128)(2,1)S(1)} collective-permute-done((bf16[4,128,128]{2,1,0:T(8,128)(2,1)S(1)}, bf16[4,128,128]{2,1,0:T(8,128)(2,1)S(1)}, u32[]{:S(2)}, u32[]{:S(2)}) %collective-permute-start.9) | collective-permute-done | bytes 131104 | tf_op jit(solution)/shard_map/ppermute | solution.py:27
  18.0 3.2 %collective-permute-done.6.refs_10_ = bf16[4,128,128]{2,1,0:T(8,128)(2,1)S(1)} collective-permute-done((bf16[4,128,128]{2,1,0:T(8,128)(2,1)S(1)}, bf16[4,128,128]{2,1,0:T(8,128)(2,1)S(1)}, u32[]{:S(2)}, u32[]{:S(2)}) %collective-permute-start.6) | collective-permute-done | bytes 131104 | tf_op jit(solution)/shard_map/ppermute | solution.py:27
  21.2 3.3 %collective-permute-done.3.refs_7_ = bf16[4,128,128]{2,1,0:T(8,128)(2,1)S(1)} collective-permute-done((bf16[4,128,128]{2,1,0:T(8,128)(2,1)S(1)}, bf16[4,128,128]{2,1,0:T(8,128)(2,1)S(1)}, u32[]{:S(2)}, u32[]{:S(2)}) %collective-permute-start.3) | collective-permute-done | bytes 131104 | tf_op jit(solution)/shard_map/ppermute | solution.py:22
  24.5 0.0 collective-permute-done.4.refs_8_
  24.5 0.0 collective-permute-done.5.refs_9_
  24.5 0.0 copy-done
  24.5 0.0 copy-done.1
  24.6 0.0 copy-done.2
  24.6 0.0 copy-done.4
  24.6 0.0 copy-start.3
  24.6 0.9 %copy-done.3 = bf16[256,256]{1,0:T(8,128)(2,1)S(1)} copy-done((bf16[256,256]{1,0:T(8,128)(2,1)S(1)}, bf16[256,256]{1,0:T(8,128)(2,1)}, u32[]{:S(2)}) %copy-start.3) | copy-done | bytes 131096
  25.5 4.4 %shard_map.55 = (f32[256,256]{1,0:T(8,128)S(1)}, f32[256,128]{1,0:T(8,128)S(1)}, bf16[1,272,256]{2,1,0:T(8,128)(2,1)S(1)}) custom-call(s32[1,1,4,4]{3,2,1,0:T(4,128)S(1)} %copy-done.4, bf16[256,256]{1,0:T(8,128)(2,1)S(1)} %copy-done.1, bf16[256,256]{1,0:T(8,128)(2,1)S(1)} %collective-permute-done.refs_1_, bf16[256,256]{1,0:T(8,128)(2,1)S(1)} %copy-done.2, ...), custom_call_target="tpu_custom_call" | custom-call | tf_op jit(solution)/shard_map/pallas_call | solution.py:176
  29.8 1.6 %collective-permute-start.10 = (bf16[272,256]{1,0:T(8,128)(2,1)S(1)}, bf16[272,256]{1,0:T(8,128)(2,1)S(1)}, u32[]{:S(2)}, u32[]{:S(2)}) collective-permute-start(bf16[272,256]{1,0:T(8,128)(2,1)S(1)} %bitcast.7), channel_id=1, source_target_pairs={{1,0},{0,1},{3,2},{2,3},{5,4},{4,5},{7,6},{6,7},{9,8},{8,9},{11,10... | collective-permute-start | bytes 417800 | tf_op jit(solution)/shard_map/ppermute | solution.py:22
  31.4 3.7 %collective-permute-done.10.refs_0_ = bf16[272,256]{1,0:T(8,128)(2,1)S(1)} collective-permute-done((bf16[272,256]{1,0:T(8,128)(2,1)S(1)}, bf16[272,256]{1,0:T(8,128)(2,1)S(1)}, u32[]{:S(2)}, u32[]{:S(2)}) %collective-permute-start.10) | collective-permute-done | bytes 139296 | tf_op jit(solution)/shard_map/ppermute | solution.py:22
  35.1 1.0 %shard_map.56 = bf16[256,256]{1,0:T(8,128)(2,1)} custom-call(f32[256,256]{1,0:T(8,128)S(1)} %get-tuple-element.8.num_ref, f32[256,128]{1,0:T(8,128)S(1)} %get-tuple-element.9.den_ref, bf16[272,256]{1,0:T(8,128)(2,1)S(1)} %collective-permute-done.10.refs_0_), custom_call_target="tpu_custom_call" | custom-call | tf_op jit(solution)/shard_map/pallas_call | solution.py:205
Async XLA Ops:
  0.0 24.5 %copy-start = (bf16[1,1,4,4,128,128]{5,4,3,2,1,0:T(8,128)(2,1)S(1)}, bf16[1,1,4,4,128,128]{5,4,3,2,1,0:T(8,128)(2,1)}, u32[]{:S(2)}) copy-start(bf16[1,1,4,4,128,128]{5,4,3,2,1,0:T(8,128)(2,1)} %refs_4_.1) | copy-start | bytes 1572868
  0.0 11.8 %collective-permute-start.1 = (bf16[256,256]{1,0:T(8,128)(2,1)}, bf16[256,256]{1,0:T(8,128)(2,1)S(1)}, u32[]{:S(2)}, u32[]{:S(2)}) collective-permute-start(bf16[256,256]{1,0:T(8,128)(2,1)} %refs_2_.1), channel_id=1, source_target_pairs={{28,0},{30,2},{0,4},{2,6},{4,8},{6,10},{8,12},{10,14},{12,16},{14,... | collective-permute-start | bytes 393224 | tf_op jit(solution)/shard_map/ppermute | solution.py:22
  2.9 11.7 %collective-permute-start.7 = (bf16[256,256]{1,0:T(8,128)(2,1)}, bf16[256,256]{1,0:T(8,128)(2,1)S(1)}, u32[]{:S(2)}, u32[]{:S(2)}) collective-permute-start(bf16[256,256]{1,0:T(8,128)(2,1)} %refs_2_.1), channel_id=1, source_target_pairs={{26,0},{0,2},{30,4},{4,6},{2,8},{8,10},{6,12},{12,14},{10,16},{16,... | collective-permute-start | bytes 393224 | tf_op jit(solution)/shard_map/ppermute | solution.py:27
  2.9 11.8 %collective-permute-start.2 = (bf16[256,256]{1,0:T(8,128)(2,1)}, bf16[256,256]{1,0:T(8,128)(2,1)S(1)}, u32[]{:S(2)}, u32[]{:S(2)}) collective-permute-start(bf16[256,256]{1,0:T(8,128)(2,1)} %refs_3_.1), channel_id=1, source_target_pairs={{28,0},{30,2},{0,4},{2,6},{4,8},{6,10},{8,12},{10,14},{12,16},{14,... | collective-permute-start | bytes 393224 | tf_op jit(solution)/shard_map/ppermute | solution.py:22
  4.5 10.3 %collective-permute-start.8 = (bf16[256,256]{1,0:T(8,128)(2,1)}, bf16[256,256]{1,0:T(8,128)(2,1)S(1)}, u32[]{:S(2)}, u32[]{:S(2)}) collective-permute-start(bf16[256,256]{1,0:T(8,128)(2,1)} %refs_3_.1), channel_id=1, source_target_pairs={{26,0},{0,2},{30,4},{4,6},{2,8},{8,10},{6,12},{12,14},{10,16},{16,... | collective-permute-start | bytes 393224 | tf_op jit(solution)/shard_map/ppermute | solution.py:27
  5.9 5.9 %collective-permute-start = (bf16[256,256]{1,0:T(8,128)(2,1)}, bf16[256,256]{1,0:T(8,128)(2,1)S(1)}, u32[]{:S(2)}, u32[]{:S(2)}) collective-permute-start(bf16[256,256]{1,0:T(8,128)(2,1)} %refs_0_.1), channel_id=1, source_target_pairs={{1,0},{0,1},{3,2},{2,3},{5,4},{4,5},{7,6},{6,7},{9,8},{8,9},{11,10... | collective-permute-start | bytes 393224 | tf_op jit(solution)/shard_map/ppermute | solution.py:22
  7.4 17.1 %copy-start.1 = (bf16[256,256]{1,0:T(8,128)(2,1)S(1)}, bf16[256,256]{1,0:T(8,128)(2,1)}, u32[]{:S(2)}) copy-start(bf16[256,256]{1,0:T(8,128)(2,1)} %refs_0_.1) | copy-start | bytes 393220
  7.4 17.1 %copy-start.2 = (bf16[256,256]{1,0:T(8,128)(2,1)S(1)}, bf16[256,256]{1,0:T(8,128)(2,1)}, u32[]{:S(2)}) copy-start(bf16[256,256]{1,0:T(8,128)(2,1)} %refs_2_.1) | copy-start | bytes 393220
  11.8 12.8 %copy-start.4 = (s32[1,1,4,4]{3,2,1,0:T(4,128)S(1)}, s32[1,1,4,4]{3,2,1,0:T(4,128)}, u32[]{:S(2)}) copy-start(s32[1,1,4,4]{3,2,1,0:T(4,128)} %tiles_ref.1) | copy-start | bytes 196
  11.8 6.2 %collective-permute-start.9 = (bf16[4,128,128]{2,1,0:T(8,128)(2,1)S(1)}, bf16[4,128,128]{2,1,0:T(8,128)(2,1)S(1)}, u32[]{:S(2)}, u32[]{:S(2)}) collective-permute-start(bf16[4,128,128]{2,1,0:T(8,128)(2,1)S(1)} %get-tuple-element.11), channel_id=1, source_target_pairs={{26,0},{0,2},{30,4},{4,6},{2,8},{8,10},{6,12},{12,14},{10,16},{16,... | collective-permute-start | bytes 393224 | tf_op jit(solution)/shard_map/ppermute | solution.py:27
  11.8 9.4 %collective-permute-start.6 = (bf16[4,128,128]{2,1,0:T(8,128)(2,1)S(1)}, bf16[4,128,128]{2,1,0:T(8,128)(2,1)S(1)}, u32[]{:S(2)}, u32[]{:S(2)}) collective-permute-start(bf16[4,128,128]{2,1,0:T(8,128)(2,1)S(1)} %get-tuple-element.12), channel_id=1, source_target_pairs={{30,0},{28,2},{2,4},{0,6},{6,8},{4,10},{10,12},{8,14},{14,16},{12,... | collective-permute-start | bytes 393224 | tf_op jit(solution)/shard_map/ppermute | solution.py:27
  14.6 9.9 %collective-permute-start.3 = (bf16[4,128,128]{2,1,0:T(8,128)(2,1)S(1)}, bf16[4,128,128]{2,1,0:T(8,128)(2,1)S(1)}, u32[]{:S(2)}, u32[]{:S(2)}) collective-permute-start(bf16[4,128,128]{2,1,0:T(8,128)(2,1)S(1)} %get-tuple-element.13), channel_id=1, source_target_pairs={{28,0},{30,2},{0,4},{2,6},{4,8},{6,10},{8,12},{10,14},{12,16},{14,... | collective-permute-start | bytes 393224 | tf_op jit(solution)/shard_map/ppermute | solution.py:22
  14.7 9.8 %collective-permute-start.4 = (bf16[256,256]{1,0:T(8,128)(2,1)S(1)}, bf16[256,256]{1,0:T(8,128)(2,1)S(1)}, u32[]{:S(2)}, u32[]{:S(2)}) collective-permute-start(bf16[256,256]{1,0:T(8,128)(2,1)S(1)} %collective-permute-done.1.refs_5_), channel_id=1, source_target_pairs={{2,0},{0,2},{6,4},{4,6},{10,8},{8,10},{14,12},{12,14},{18,16},{16,... | collective-permute-start | bytes 393224 | tf_op jit(solution)/shard_map/ppermute | solution.py:27
  14.8 9.8 %collective-permute-start.5 = (bf16[256,256]{1,0:T(8,128)(2,1)S(1)}, bf16[256,256]{1,0:T(8,128)(2,1)S(1)}, u32[]{:S(2)}, u32[]{:S(2)}) collective-permute-start(bf16[256,256]{1,0:T(8,128)(2,1)S(1)} %collective-permute-done.2.refs_6_), channel_id=1, source_target_pairs={{2,0},{0,2},{6,4},{4,6},{10,8},{8,10},{14,12},{12,14},{18,16},{16,... | collective-permute-start | bytes 393224 | tf_op jit(solution)/shard_map/ppermute | solution.py:27
  24.6 0.9 %copy-start.3 = (bf16[256,256]{1,0:T(8,128)(2,1)S(1)}, bf16[256,256]{1,0:T(8,128)(2,1)}, u32[]{:S(2)}) copy-start(bf16[256,256]{1,0:T(8,128)(2,1)} %refs_3_.1) | copy-start | bytes 393220
  29.8 5.2 %collective-permute-start.10 = (bf16[272,256]{1,0:T(8,128)(2,1)S(1)}, bf16[272,256]{1,0:T(8,128)(2,1)S(1)}, u32[]{:S(2)}, u32[]{:S(2)}) collective-permute-start(bf16[272,256]{1,0:T(8,128)(2,1)S(1)} %bitcast.7), channel_id=1, source_target_pairs={{1,0},{0,1},{3,2},{2,3},{5,4},{4,5},{7,6},{6,7},{9,8},{8,9},{11,10... | collective-permute-start | bytes 417800 | tf_op jit(solution)/shard_map/ppermute | solution.py:22

commit v2 on v1

v2 whole, which is shorter than its diff:
```python
import functools
import math

import jax
import jax.numpy as jnp
from jax import lax
from jax.experimental import pallas as pl
from jax.experimental.pallas import tpu as pltpu
from jax.sharding import PartitionSpec as P

HEADS = 4
LEAKY_SLOPE = 0.2
CORES = 2
UNROLL = 4
EXTRA_ROWS = 16
LANES = 128
VMEM_BYTES = 16 * 2**20
WHOLE = pl.BlockSpec(memory_space=pltpu.VMEM)
ANYWHERE = pl.BlockSpec(memory_space=pltpu.HBM)
PARAMS = pltpu.CompilerParams(vmem_limit_bytes=VMEM_BYTES)
SHORT = pl.CostEstimate(flops=1, bytes_accessed=1, transcendentals=0)


def moved(block, axis, distance):
    count = lax.axis_size(axis)
    return lax.ppermute(block, axis, [((i - distance) % count, i) for i in range(count)])


def routed(block, source_of):
    count = lax.axis_size("blk")
    return lax.ppermute(block, "blk", [(source_of(i) % count, i) for i in range(count)])


def core_of_blk():
    return lax.rem(lax.axis_index("blk"), CORES)


def pack_kernel(key_ref, value_ref, edges_ref, *refs, lists):
    *outs, sem = refs
    rows, feats = key_ref.shape
    list_rows = edges_ref.shape[1]
    core = core_of_blk()
    copies = []
    for out_ref, (with_block, stops) in zip(outs, lists):
        at = 0
        if with_block:
            for ref in (key_ref, value_ref):
                for c in range(0, feats, LANES):
                    copies.append((ref.at[:, c : c + LANES], out_ref.at[at : at + rows, :]))
                    at += rows
        for stop in stops:
            copies.append((edges_ref.at[stop(core)], out_ref.at[at : at + list_rows, :]))
            at += list_rows
    running = [pltpu.make_async_copy(a, b, sem.at[n]) for n, (a, b) in enumerate(copies)]
    for copy in running:
        copy.start()
    for copy in running:
        copy.wait()


def packed(keys, values, edges, lists):
    rows, feats = keys.shape
    capacity, tile = edges.shape[3], edges.shape[4]
    block = 2 * feats // LANES
    sizes = [(block * rows if with_block else 0) + len(stops) * capacity * tile for with_block, stops in lists]
    count = sum((block if with_block else 0) + len(stops) for with_block, stops in lists)
    return pl.pallas_call(
        functools.partial(pack_kernel, lists=lists),
        in_specs=[ANYWHERE] * 3,
        out_specs=[WHOLE] * len(lists),
        out_shape=[jax.ShapeDtypeStruct((size, LANES), jnp.bfloat16) for size in sizes],
        scratch_shapes=[pltpu.SemaphoreType.DMA((count,))],
        compiler_params=PARAMS,
        cost_estimate=SHORT,
    )(*[pltpu.with_memory_space_constraint(x, pltpu.HBM) for x in (keys, values, edges.reshape(edges.shape[2], capacity * tile, tile))])


def head_masked(block, head_count):
    head_dim = block.shape[1] // head_count
    head_of = lax.broadcasted_iota(jnp.int32, block.shape, 1) // head_dim
    return jnp.concatenate(
        [jnp.where(head_of == h, block, jnp.zeros_like(block)) for h in range(head_count)], axis=0
    )


def tile_of(part, c, rows, tile, feats):
    ref, at = part
    wide = ref.shape[1]
    starts = [at + piece * rows + c * tile for piece in range(feats // wide)]
    return jnp.concatenate([ref[s : s + tile, :] for s in starts], axis=1)


def add_stop(n, tiles_ref, stop, keys, values, edges, query_ref, sums_ref, squares_ref, stack_ref, sizes):
    fibers, key_tiles, tile, scale = sizes
    capacity = tiles_ref.shape[-1]
    group = math.gcd(capacity, UNROLL)
    fiber = lax.axis_index("fiber")
    tall = HEADS * tile
    lane = lax.broadcasted_iota(jnp.int32, (tile, LANES), 1)
    for c in range(key_tiles):
        stack_ref[2 * n, c * tall : (c + 1) * tall, :] = head_masked(tile_of(keys, c, key_tiles * tile, tile, query_ref.shape[1]), HEADS)
        stack_ref[2 * n + 1, c * tall : (c + 1) * tall, :] = head_masked(tile_of(values, c, key_tiles * tile, tile, query_ref.shape[1]), HEADS)

    def one_group(g, carry):
        for k in range(group):
            slot = g * group + k
            listed = tiles_ref[0, 0, stop, slot]
            number = jnp.maximum(listed, 0)
            row_tile = lax.div(number, key_tiles)
            col_tile = lax.rem(number, key_tiles)
            part = lax.rem(lax.div(row_tile, key_tiles) - fiber + fibers, fibers)
            at = pl.multiple_of((part * key_tiles + lax.rem(row_tile, key_tiles)) * tile, tile)
            stack = pl.ds(pl.multiple_of(col_tile * tall, tall), tall)
            scores = lax.dot_general(
                query_ref[pl.ds(at, tile), :],
                stack_ref[2 * n, stack, :],
                (((1,), (1,)), ((), ())),
                preferred_element_type=jnp.float32,
            )
            edge_rows = pl.ds(edges[1] + slot * tile, tile)
            if not isinstance(slot, int):
                edge_rows = pl.ds(pl.multiple_of(edges[1] + slot * tile, tile), tile)
            edge = jnp.where(listed >= 0, edges[0][edge_rows, :].astype(jnp.float32) * scale, 0.0)
            weights = jnp.maximum(scores, LEAKY_SLOPE * scores) * jnp.concatenate([edge] * HEADS, axis=1)
            squared = weights * weights
            den = jnp.zeros((tile, LANES), jnp.float32)
            for h in range(HEADS):
                total = jnp.sum(squared[:, h * tile : (h + 1) * tile], axis=1, keepdims=True)
                den = jnp.where(lane == h, total, den)
            squares_ref[pl.ds(at, tile), :] += den
            sums_ref[pl.ds(at, tile), :] += jnp.dot(
                weights.astype(jnp.bfloat16), stack_ref[2 * n + 1, stack, :], preferred_element_type=jnp.float32
            )
        return carry

    if capacity == group:
        one_group(0, 0)
    else:
        lax.fori_loop(0, capacity // group, one_group, 0)


def first_kernel(tiles_ref, *refs, plan, packets, sizes):
    fibers, key_tiles, tile, scale = sizes
    queries, arrived = refs[:fibers], refs[fibers : fibers + packets]
    query_ref, sums_ref, squares_ref, stack_ref = refs[fibers + packets :]
    rows = key_tiles * tile
    for r in range(fibers):
        query_ref[r * rows : (r + 1) * rows, :] = queries[r][...]
    sums_ref[...] = jnp.zeros_like(sums_ref)
    squares_ref[...] = jnp.zeros_like(squares_ref)
    add_plan(tiles_ref, plan, arrived, query_ref, sums_ref, squares_ref, stack_ref, sizes)


def add_plan(tiles_ref, plan, arrived, query_ref, sums_ref, squares_ref, stack_ref, sizes):
    core = core_of_blk()
    for n, (stop, *parts) in enumerate(plan):
        parts = [(arrived[packet], at) for packet, at in parts]
        add_stop(n, tiles_ref, stop(core), *parts, query_ref, sums_ref, squares_ref, stack_ref, sizes)


def more_kernel(tiles_ref, query_ref, sums_in, squares_in, *refs, plan, packets, sizes):
    arrived = refs[:packets]
    sums_ref, squares_ref, stack_ref = refs[packets:]
    sums_ref[...] = sums_in[...]
    squares_ref[...] = squares_in[...]
    add_plan(tiles_ref, plan, arrived, query_ref, sums_ref, squares_ref, stack_ref, sizes)


def last_kernel(tiles_ref, query_ref, sums_in, squares_in, *refs, plan, packets, sizes):
    arrived = refs[:packets]
    num_ref, den_ref, payload_ref, stack_ref, sums_ref, squares_ref = refs[packets:]
    sums_ref[...] = sums_in[...]
    squares_ref[...] = squares_in[...]
    add_plan(tiles_ref, plan, arrived, query_ref, sums_ref, squares_ref, stack_ref, sizes)
    hand_out(sums_ref, squares_ref, num_ref, den_ref, payload_ref, sizes)


def hand_out(sums_ref, squares_ref, num_ref, den_ref, payload_ref, sizes):
    fibers, key_tiles, tile, scale = sizes
    rows = key_tiles * tile
    half = EXTRA_ROWS // 2
    for r in range(1, fibers):
        payload_ref[r - 1, :rows, :] = sums_ref[r * rows : (r + 1) * rows, :].astype(jnp.bfloat16)
        for t in range(key_tiles):
            den = squares_ref[r * rows + t * tile : r * rows + (t + 1) * tile, :]
            high = den.astype(jnp.bfloat16)
            rest = den - high.astype(jnp.float32)
            both = jnp.concatenate([high.astype(jnp.float32).T[:half], rest.T[:half]], axis=0)
            payload_ref[r - 1, rows : rows + EXTRA_ROWS, t * tile : (t + 1) * tile] = both.astype(jnp.bfloat16)
    num_ref[...] = sums_ref[:rows, :]
    den_ref[...] = squares_ref[:rows, :]


def finish_kernel(num_ref, den_ref, *refs, sizes):
    fibers, key_tiles, tile, scale = sizes
    *payloads, out_ref = refs
    rows, feats = num_ref.shape
    head_dim = feats // HEADS
    half = EXTRA_ROWS // 2
    head_of = lax.broadcasted_iota(jnp.int32, (tile, feats), 1) // head_dim
    for t in range(key_tiles):
        here = slice(t * tile, (t + 1) * tile)
        num = num_ref[here, :]
        den = den_ref[here, :]
        for payload in payloads:
            num = num + payload[here, :].astype(jnp.float32)
            both = payload[rows : rows + EXTRA_ROWS, here].astype(jnp.float32)
            total = both[:half] + both[half:]
            padded = jnp.concatenate([total, jnp.zeros((LANES - half, tile), jnp.float32)], axis=0)
            den = den + padded.T
        spread = lax.rsqrt(1.0 + den)
        factor = jnp.broadcast_to(spread[:, 0:1], (tile, feats))
        for h in range(1, HEADS):
            factor = jnp.where(head_of == h, spread[:, h : h + 1], factor)
        out_ref[here, :] = (num * factor).astype(jnp.bfloat16)


def on_device(queries, keys, values, tiles, edges):
    fibers = lax.axis_size("fiber")
    rows, feats = keys.shape
    stops, capacity, tile = tiles.shape[2], tiles.shape[3], edges.shape[-1]
    key_tiles = rows // tile
    scale = (feats // HEADS) ** (-0.5) * (stops * fibers * rows / 4) ** (-0.5)
    sizes = (fibers, key_tiles, tile, scale)
    half_rows = feats // LANES * rows
    list_rows = capacity * tile

    shifts = range(CORES, stops, CORES)
    far = [moved((keys, values), "blk", s) for s in shifts]
    own, odd, *pairs = packed(
        keys, values, edges,
        [
            (True, [lambda core: 0]),
            (True, [lambda core: jnp.where(core == 1, stops - 1, 1)]),
        ]
        + [(False, [lambda core, s=s: jnp.where(core == 1, s - 1, s + 1), lambda core, s=s: s]) for s in shifts],
    )
    near = [routed(block, lambda i: i ^ 1) for block in far]
    pairs = [moved(pair, "blk", s) for pair, s in zip(pairs, shifts)]
    odd = routed(odd, lambda i: i - 1 if i % CORES else i - stops + 1)
    all_queries = [queries] + [moved(queries, "fiber", -r) for r in range(1, fibers)]

    smem = pl.BlockSpec(memory_space=pltpu.SMEM)
    state = [
        jax.ShapeDtypeStruct((fibers * rows, feats), jnp.bfloat16),
        jax.ShapeDtypeStruct((fibers * rows, feats), jnp.float32),
        jax.ShapeDtypeStruct((fibers * rows, LANES), jnp.float32),
    ]

    def stack(count):
        return pltpu.VMEM((2 * count, key_tiles * HEADS * tile, feats), jnp.bfloat16)

    plan = [(lambda core: 0, (0, 0), (0, half_rows), (0, 2 * half_rows))]
    all_q, sums, squares = pl.pallas_call(
        functools.partial(first_kernel, plan=plan, packets=1, sizes=sizes),
        in_specs=[smem] + [WHOLE] * (1 + fibers),
        out_specs=[WHOLE] * 3,
        out_shape=state,
        scratch_shapes=[stack(len(plan))],
        compiler_params=PARAMS,
        cost_estimate=SHORT,
    )(tiles, *all_queries, own)
    pairs, near, all_q, sums, squares = lax.optimization_barrier((pairs, near, all_q, sums, squares))
    arrived, plan = [], []
    for s, pair, far_block, near_block in zip(shifts, pairs, far, near):
        at = len(arrived)
        arrived += [*far_block, pair, *near_block, routed(pair, lambda i: i ^ 1)]
        plan.append((lambda core, s=s: s, (at, 0), (at + 1, 0), (at + 2, list_rows)))
        plan.append((lambda core, s=s: jnp.where(core == 0, s - 1, s + 1), (at + 3, 0), (at + 4, 0), (at + 5, 0)))
    sums, squares = pl.pallas_call(
        functools.partial(more_kernel, plan=plan, packets=len(arrived), sizes=sizes),
        in_specs=[smem] + [WHOLE] * (3 + len(arrived)),
        out_specs=[WHOLE] * 2,
        out_shape=state[1:],
        scratch_shapes=[stack(len(plan))],
        compiler_params=PARAMS,
        cost_estimate=SHORT,
    )(tiles, all_q, sums, squares, *arrived)
    arrived = [odd]
    plan = [(lambda core: jnp.where(core == 0, stops - 1, 1), (0, 0), (0, half_rows), (0, 2 * half_rows))]
    num, den, payload = pl.pallas_call(
        functools.partial(last_kernel, plan=plan, packets=len(arrived), sizes=sizes),
        in_specs=[smem] + [WHOLE] * (3 + len(arrived)),
        out_specs=[WHOLE] * 3,
        out_shape=[
            jax.ShapeDtypeStruct((rows, feats), jnp.float32),
            jax.ShapeDtypeStruct((rows, LANES), jnp.float32),
            jax.ShapeDtypeStruct((max(fibers - 1, 1), rows + EXTRA_ROWS, feats), jnp.bfloat16),
        ],
        scratch_shapes=[stack(len(plan)), pltpu.VMEM(state[1].shape, jnp.float32), pltpu.VMEM(state[2].shape, jnp.float32)],
        compiler_params=PARAMS,
        cost_estimate=SHORT,
    )(tiles, all_q, sums, squares, *arrived)
    partials = [moved(payload[r - 1], "fiber", r) for r in range(1, fibers)]
    return pl.pallas_call(
        functools.partial(finish_kernel, sizes=sizes),
        in_specs=[WHOLE] * (2 + len(partials)),
        out_specs=WHOLE,
        out_shape=jax.ShapeDtypeStruct((rows, feats), jnp.bfloat16),
        compiler_params=PARAMS,
        cost_estimate=SHORT,
    )(num, den, *partials)


def solution(mesh):
    return jax.shard_map(
        on_device,
        mesh=mesh,
        in_specs=(
            P(("blk", "fiber"), None),
            P(("blk", "fiber"), None),
            P(("blk", "fiber"), None),
            P("blk", "fiber", None, None),
            P("blk", "fiber", None, None, None, None),
        ),
        out_specs=P(("blk", "fiber"), None),
        check_vma=False,
    )
```

time: 36.2 us -> 31.6 us (0.87)
  waiting for transfers between devices: 16.2 us -> 13.2 us
  Pallas kernels: 5.32 us -> 8.26 us
  starting transfers between devices: 12.4 us -> 9.87 us
  local copies, waits for them, and re-layouts: 2.01 us -> 0.01 us
    ppermute x6 -> x4, waiting for transfers between devices: 6 us -> 1.54 us  [routed(): lax.ppermute(block, 'blk', [(source_of(i) % count, i) for i in range(coun...]
    ppermute x6 -> x4, starting transfers between devices: 4.71 us -> 0.52 us  [routed(): lax.ppermute(block, 'blk', [(source_of(i) % count, i) for i in range(coun...]
    pallas_call x2 -> x5, Pallas kernels: 5.32 us -> 8.26 us  [the longest x1 2.51 us: on_device(): pl.pallas_call(functools.partial(more_kernel, plan=plan, packets=len(arri...]
    ppermute x5, starting transfers between devices: 7.67 us -> 9.35 us  [moved(): lax.ppermute(block, axis, [((i - distance) % count, i) for i in range(cou...]
    ppermute x5, waiting for transfers between devices: 10.2 us -> 11.7 us  [moved(): lax.ppermute(block, axis, [((i - distance) % count, i) for i in range(cou...]
    squeeze x1 -> x0, local copies, waits for them, and re-layouts: 1.1 us -> none  [edges_of(): return lax.dynamic_index_in_dim(own_edges, stop, 0, keepdims=False)]
    unnamed x10 -> x4, local copies, waits for them, and re-layouts: 0.91 us -> 0.01 us
  transfers between devices with their start and end apart: 11 -> 9, of which waited for: 5 -> 5; matrix products, arithmetic and copies ran while one was open for 3% -> 0% of each run, Pallas kernels for 0% -> 18%
where the time goes in v2:
time: 31.6 us; the launch traced here: 31.4 us
  waiting for transfers between devices  13.2 us (42%)
  starting transfers between devices  9.87 us (31%)
  Pallas kernels  8.26 us (26%)
    ppermute x5, waiting for transfers between devices, moved(): lax.ppermute(block, axis, [((i - distance) % count, i) for i in range(cou...  11.7 us
    ppermute x5, starting transfers between devices, moved(): lax.ppermute(block, axis, [((i - distance) % count, i) for i in range(cou...  9.35 us
    pallas_call x1, Pallas kernels, on_device(): pl.pallas_call(functools.partial(more_kernel, plan=plan, packets=len(arri...  2.51 us
    pallas_call x1, Pallas kernels, on_device(): pl.pallas_call(functools.partial(last_kernel, plan=plan, packets=len(arri...  1.69 us
    pallas_call x1, Pallas kernels, on_device(): pl.pallas_call(functools.partial(first_kernel, plan=plan, packets=1, size...  1.67 us
    ppermute x4, waiting for transfers between devices, routed(): lax.ppermute(block, 'blk', [(source_of(i) % count, i) for i in range(coun...  1.54 us
    pallas_call x1, Pallas kernels, packed(): pl.pallas_call(functools.partial(pack_kernel, lists=lists), in_specs=[ANY...  1.42 us
    pallas_call x1, Pallas kernels, on_device(): pl.pallas_call(functools.partial(finish_kernel, sizes=sizes), in_specs=[W...  0.96 us
  transfers between devices with their start and end apart: 9, of which 5 were waited for; matrix products, arithmetic and copies ran while one was open for 0% of the time, Pallas kernels for 18%

profile of v2, /device:TPU:0, one launch (start us, length us, event | category | flops | bytes accessed | tf_op | source)
XLA Modules:
  0.0 31.4 jit_solution(10369010062278338163)
XLA Ops:
  0.0 2.9 %collective-permute-start.1 = (bf16[256,256]{1,0:T(8,128)(2,1)}, bf16[256,256]{1,0:T(8,128)(2,1)S(1)}, u32[]{:S(2)}, u32[]{:S(2)}) collective-permute-start(bf16[256,256]{1,0:T(8,128)(2,1)} %key_ref.1), channel_id=1, source_target_pairs={{28,0},{30,2},{0,4},{2,6},{4,8},{6,10},{8,12},{10,14},{12,16},{14,... | collective-permute-start | bytes 393224 | tf_op jit(solution)/shard_map/ppermute | solution.py:26
  2.9 1.5 %collective-permute-start.3 = (bf16[256,256]{1,0:T(8,128)(2,1)}, bf16[256,256]{1,0:T(8,128)(2,1)S(1)}, u32[]{:S(2)}, u32[]{:S(2)}) collective-permute-start(bf16[256,256]{1,0:T(8,128)(2,1)} %value_ref.1), channel_id=1, source_target_pairs={{28,0},{30,2},{0,4},{2,6},{4,8},{6,10},{8,12},{10,14},{12,16},{14,... | collective-permute-start | bytes 393224 | tf_op jit(solution)/shard_map/ppermute | solution.py:26
  4.5 0.0 copy-start
  4.5 1.4 %shard_map.55 = (bf16[1536,128]{1,0:T(8,128)(2,1)S(1)}, bf16[1536,128]{1,0:T(8,128)(2,1)S(1)}, bf16[1024,128]{1,0:T(8,128)(2,1)S(1)}) custom-call(bf16[256,256]{1,0:T(8,128)(2,1)} %key_ref.1, bf16[256,256]{1,0:T(8,128)(2,1)} %value_ref.1, bf16[4,512,128]{2,1,0:T(8,128)(2,1)} %bitcast.3), custom_call_target="tpu_custom_call" | custom-call | flops 1 | bytes 1 | tf_op jit(solution)/shard_map/pallas_call | solution.py:67
  5.9 0.0 copy-start.1
  5.9 1.5 %collective-permute-start = (bf16[1024,128]{1,0:T(8,128)(2,1)S(1)}, bf16[1024,128]{1,0:T(8,128)(2,1)S(1)}, u32[]{:S(2)}, u32[]{:S(2)}) collective-permute-start(bf16[1024,128]{1,0:T(8,128)(2,1)S(1)} %get-tuple-element.22), channel_id=1, source_target_pairs={{28,0},{30,2},{0,4},{2,6},{4,8},{6,10},{8,12},{10,14},{12,16},{14,... | collective-permute-start | bytes 786440 | tf_op jit(solution)/shard_map/ppermute | solution.py:26
  7.5 0.0 copy-done
  7.5 1.5 %collective-permute-start.5 = (bf16[256,256]{1,0:T(8,128)(2,1)S(1)}, bf16[256,256]{1,0:T(8,128)(2,1)S(1)}, u32[]{:S(2)}, u32[]{:S(2)}) collective-permute-start(bf16[256,256]{1,0:T(8,128)(2,1)S(1)} %copy-done), channel_id=1, source_target_pairs={{1,0},{0,1},{3,2},{2,3},{5,4},{4,5},{7,6},{6,7},{9,8},{8,9},{11,10... | collective-permute-start | bytes 393224 | tf_op jit(solution)/shard_map/ppermute | solution.py:26
  9.0 1.5 %collective-permute-done.1.refs_0_ = bf16[256,256]{1,0:T(8,128)(2,1)S(1)} collective-permute-done((bf16[256,256]{1,0:T(8,128)(2,1)}, bf16[256,256]{1,0:T(8,128)(2,1)S(1)}, u32[]{:S(2)}, u32[]{:S(2)}) %collective-permute-start.1) | collective-permute-done | bytes 131104 | tf_op jit(solution)/shard_map/ppermute | solution.py:26
  10.5 0.0 collective-permute-start.2
  10.5 2.8 %collective-permute-done.3.refs_1_ = bf16[256,256]{1,0:T(8,128)(2,1)S(1)} collective-permute-done((bf16[256,256]{1,0:T(8,128)(2,1)}, bf16[256,256]{1,0:T(8,128)(2,1)S(1)}, u32[]{:S(2)}, u32[]{:S(2)}) %collective-permute-start.3) | collective-permute-done | bytes 131104 | tf_op jit(solution)/shard_map/ppermute | solution.py:26
  13.3 0.0 collective-permute-start.4
  13.3 0.5 %collective-permute-start.7 = (bf16[1536,128]{1,0:T(8,128)(2,1)S(1)}, bf16[1536,128]{1,0:T(8,128)(2,1)S(1)}, u32[]{:S(2)}, u32[]{:S(2)}) collective-permute-start(bf16[1536,128]{1,0:T(8,128)(2,1)S(1)} %get-tuple-element.35), channel_id=1, source_target_pairs={{26,0},{0,2},{30,4},{4,6},{2,8},{8,10},{6,12},{12,14},{10,16},{16,... | collective-permute-start | bytes 1179656 | tf_op jit(solution)/shard_map/ppermute | solution.py:31
  13.8 0.0 collective-permute-done.5.refs_1_
  13.8 0.0 copy-done.1
  13.8 1.7 %shard_map.56 = (bf16[512,256]{1,0:T(8,128)(2,1)S(1)}, f32[512,256]{1,0:T(8,128)S(1)}, f32[512,128]{1,0:T(8,128)S(1)}) custom-call(s32[1,1,4,4]{3,2,1,0:T(4,128)S(1)} %copy-done.1, bf16[256,256]{1,0:T(8,128)(2,1)S(1)} %copy-done, bf16[256,256]{1,0:T(8,128)(2,1)S(1)} %collective-permute-done.5.refs_1_, bf16[1536,128]{1,0:T(8,128)(2,1)S(1)} %get-tuple-element.23.refs_2_), custom_call_target="tpu_custom_call" | custom-call | flops 1 | bytes 1 | tf_op jit(solution)/shard_map/pallas_call | solution.py:254
  15.5 0.0 collective-permute-done.2.refs_3_
  15.5 0.0 collective-permute-done.4.refs_4_
  15.5 3.4 %collective-permute-done.refs_2_ = bf16[1024,128]{1,0:T(8,128)(2,1)S(1)} collective-permute-done((bf16[1024,128]{1,0:T(8,128)(2,1)S(1)}, bf16[1024,128]{1,0:T(8,128)(2,1)S(1)}, u32[]{:S(2)}, u32[]{:S(2)}) %collective-permute-start) | collective-permute-done | bytes 262176 | tf_op jit(solution)/shard_map/ppermute | solution.py:26
  18.9 0.0 collective-permute-start.6
  18.9 1.5 %collective-permute-done.6.refs_5_ = bf16[1024,128]{1,0:T(8,128)(2,1)S(1)} collective-permute-done((bf16[1024,128]{1,0:T(8,128)(2,1)S(1)}, bf16[1024,128]{1,0:T(8,128)(2,1)S(1)}, u32[]{:S(2)}, u32[]{:S(2)}) %collective-permute-start.6) | collective-permute-done | bytes 262176 | tf_op jit(solution)/shard_map/ppermute | solution.py:31
  20.5 2.5 %shard_map.57 = (f32[512,256]{1,0:T(8,128)S(1)}, f32[512,128]{1,0:T(8,128)S(1)}) custom-call(s32[1,1,4,4]{3,2,1,0:T(4,128)S(1)} %copy-done.1, bf16[512,256]{1,0:T(8,128)(2,1)S(1)} %get-tuple-element.27.query_ref, f32[512,256]{1,0:T(8,128)S(1)} %get-tuple-element.28.sums_in, f32[512,128]{1,0:T(8,128)S(1)} %get-tuple-element.29.squares_in, ...), custom_call_target="tpu_custom_call" | custom-call | flops 1 | bytes 1 | tf_op jit(solution)/shard_map/pallas_call | solution.py:270
  23.0 0.0 collective-permute-done.7.refs_0_
  23.0 1.7 %shard_map.58 = (f32[256,256]{1,0:T(8,128)S(1)}, f32[256,128]{1,0:T(8,128)S(1)}, bf16[1,272,256]{2,1,0:T(8,128)(2,1)S(1)}) custom-call(s32[1,1,4,4]{3,2,1,0:T(4,128)S(1)} %copy-done.1, bf16[512,256]{1,0:T(8,128)(2,1)S(1)} %get-tuple-element.27.query_ref, f32[512,256]{1,0:T(8,128)S(1)} %get-tuple-element.33.sums_in, ...), custom_call_target="tpu_custom_call" | custom-call | flops 1 | bytes 1 | tf_op jit(solution)/shard_map/pallas_call | solution.py:281
  24.7 1.8 %collective-permute-start.8 = (bf16[272,256]{1,0:T(8,128)(2,1)S(1)}, bf16[272,256]{1,0:T(8,128)(2,1)S(1)}, u32[]{:S(2)}, u32[]{:S(2)}) collective-permute-start(bf16[272,256]{1,0:T(8,128)(2,1)S(1)} %bitcast.2), channel_id=1, source_target_pairs={{1,0},{0,1},{3,2},{2,3},{5,4},{4,5},{7,6},{6,7},{9,8},{8,9},{11,10... | collective-permute-start | bytes 417800 | tf_op jit(solution)/shard_map/ppermute | solution.py:26
  26.5 4.0 %collective-permute-done.8.refs_0_ = bf16[272,256]{1,0:T(8,128)(2,1)S(1)} collective-permute-done((bf16[272,256]{1,0:T(8,128)(2,1)S(1)}, bf16[272,256]{1,0:T(8,128)(2,1)S(1)}, u32[]{:S(2)}, u32[]{:S(2)}) %collective-permute-start.8) | collective-permute-done | bytes 139296 | tf_op jit(solution)/shard_map/ppermute | solution.py:26
  30.5 1.0 %shard_map.59 = bf16[256,256]{1,0:T(8,128)(2,1)} custom-call(f32[256,256]{1,0:T(8,128)S(1)} %get-tuple-element.36.num_ref, f32[256,128]{1,0:T(8,128)S(1)} %get-tuple-element.37.den_ref, bf16[272,256]{1,0:T(8,128)(2,1)S(1)} %collective-permute-done.8.refs_0_), custom_call_target="tpu_custom_call" | custom-call | flops 1 | bytes 1 | tf_op jit(solution)/shard_map/pallas_call | solution.py:295
Async XLA Ops:
  0.0 10.5 %collective-permute-start.1 = (bf16[256,256]{1,0:T(8,128)(2,1)}, bf16[256,256]{1,0:T(8,128)(2,1)S(1)}, u32[]{:S(2)}, u32[]{:S(2)}) collective-permute-start(bf16[256,256]{1,0:T(8,128)(2,1)} %key_ref.1), channel_id=1, source_target_pairs={{28,0},{30,2},{0,4},{2,6},{4,8},{6,10},{8,12},{10,14},{12,16},{14,... | collective-permute-start | bytes 393224 | tf_op jit(solution)/shard_map/ppermute | solution.py:26
  2.9 10.4 %collective-permute-start.3 = (bf16[256,256]{1,0:T(8,128)(2,1)}, bf16[256,256]{1,0:T(8,128)(2,1)S(1)}, u32[]{:S(2)}, u32[]{:S(2)}) collective-permute-start(bf16[256,256]{1,0:T(8,128)(2,1)} %value_ref.1), channel_id=1, source_target_pairs={{28,0},{30,2},{0,4},{2,6},{4,8},{6,10},{8,12},{10,14},{12,16},{14,... | collective-permute-start | bytes 393224 | tf_op jit(solution)/shard_map/ppermute | solution.py:26
  4.5 3.0 %copy-start = (bf16[256,256]{1,0:T(8,128)(2,1)S(1)}, bf16[256,256]{1,0:T(8,128)(2,1)}, u32[]{:S(2)}) copy-start(bf16[256,256]{1,0:T(8,128)(2,1)} %refs_0_.1) | copy-start | bytes 393220
  5.9 7.9 %copy-start.1 = (s32[1,1,4,4]{3,2,1,0:T(4,128)S(1)}, s32[1,1,4,4]{3,2,1,0:T(4,128)}, u32[]{:S(2)}) copy-start(s32[1,1,4,4]{3,2,1,0:T(4,128)} %tiles_ref.5) | copy-start | bytes 196
  5.9 13.0 %collective-permute-start = (bf16[1024,128]{1,0:T(8,128)(2,1)S(1)}, bf16[1024,128]{1,0:T(8,128)(2,1)S(1)}, u32[]{:S(2)}, u32[]{:S(2)}) collective-permute-start(bf16[1024,128]{1,0:T(8,128)(2,1)S(1)} %get-tuple-element.22), channel_id=1, source_target_pairs={{28,0},{30,2},{0,4},{2,6},{4,8},{6,10},{8,12},{10,14},{12,16},{14,... | collective-permute-start | bytes 786440 | tf_op jit(solution)/shard_map/ppermute | solution.py:26
  7.5 6.4 %collective-permute-start.5 = (bf16[256,256]{1,0:T(8,128)(2,1)S(1)}, bf16[256,256]{1,0:T(8,128)(2,1)S(1)}, u32[]{:S(2)}, u32[]{:S(2)}) collective-permute-start(bf16[256,256]{1,0:T(8,128)(2,1)S(1)} %copy-done), channel_id=1, source_target_pairs={{1,0},{0,1},{3,2},{2,3},{5,4},{4,5},{7,6},{6,7},{9,8},{8,9},{11,10... | collective-permute-start | bytes 393224 | tf_op jit(solution)/shard_map/ppermute | solution.py:26
  10.5 5.0 %collective-permute-start.2 = (bf16[256,256]{1,0:T(8,128)(2,1)S(1)}, bf16[256,256]{1,0:T(8,128)(2,1)S(1)}, u32[]{:S(2)}, u32[]{:S(2)}) collective-permute-start(bf16[256,256]{1,0:T(8,128)(2,1)S(1)} %collective-permute-done.1.refs_0_), channel_id=1, source_target_pairs={{2,0},{0,2},{6,4},{4,6},{10,8},{8,10},{14,12},{12,14},{18,16},{16,... | collective-permute-start | bytes 393224 | tf_op jit(solution)/shard_map/ppermute | solution.py:31
  13.3 2.2 %collective-permute-start.4 = (bf16[256,256]{1,0:T(8,128)(2,1)S(1)}, bf16[256,256]{1,0:T(8,128)(2,1)S(1)}, u32[]{:S(2)}, u32[]{:S(2)}) collective-permute-start(bf16[256,256]{1,0:T(8,128)(2,1)S(1)} %collective-permute-done.3.refs_1_), channel_id=1, source_target_pairs={{2,0},{0,2},{6,4},{4,6},{10,8},{8,10},{14,12},{12,14},{18,16},{16,... | collective-permute-start | bytes 393224 | tf_op jit(solution)/shard_map/ppermute | solution.py:31
  13.3 9.7 %collective-permute-start.7 = (bf16[1536,128]{1,0:T(8,128)(2,1)S(1)}, bf16[1536,128]{1,0:T(8,128)(2,1)S(1)}, u32[]{:S(2)}, u32[]{:S(2)}) collective-permute-start(bf16[1536,128]{1,0:T(8,128)(2,1)S(1)} %get-tuple-element.35), channel_id=1, source_target_pairs={{26,0},{0,2},{30,4},{4,6},{2,8},{8,10},{6,12},{12,14},{10,16},{16,... | collective-permute-start | bytes 1179656 | tf_op jit(solution)/shard_map/ppermute | solution.py:31
  18.9 1.5 %collective-permute-start.6 = (bf16[1024,128]{1,0:T(8,128)(2,1)S(1)}, bf16[1024,128]{1,0:T(8,128)(2,1)S(1)}, u32[]{:S(2)}, u32[]{:S(2)}) collective-permute-start(bf16[1024,128]{1,0:T(8,128)(2,1)S(1)} %collective-permute-done.refs_2_), channel_id=1, source_target_pairs={{2,0},{0,2},{6,4},{4,6},{10,8},{8,10},{14,12},{12,14},{18,16},{16,... | collective-permute-start | bytes 786440 | tf_op jit(solution)/shard_map/ppermute | solution.py:31
  24.7 5.8 %collective-permute-start.8 = (bf16[272,256]{1,0:T(8,128)(2,1)S(1)}, bf16[272,256]{1,0:T(8,128)(2,1)S(1)}, u32[]{:S(2)}, u32[]{:S(2)}) collective-permute-start(bf16[272,256]{1,0:T(8,128)(2,1)S(1)} %bitcast.2), channel_id=1, source_target_pairs={{1,0},{0,1},{3,2},{2,3},{5,4},{4,5},{7,6},{6,7},{9,8},{8,9},{11,10... | collective-permute-start | bytes 417800 | tf_op jit(solution)/shard_map/ppermute | solution.py:26

commit v3 on v2

--- a/solution.py
+++ b/solution.py
@@ -90,16 +90,32 @@
     return jnp.concatenate([ref[s : s + tile, :] for s in starts], axis=1)
 
 
+def stack_keys(key_stack, at, block):
+    feats, tile = block.shape[1], block.shape[0]
+    turned = block.T
+    head_of = lax.broadcasted_iota(jnp.int32, (feats, tile), 0) // (feats // HEADS)
+    key_stack[at] = jnp.concatenate(
+        [jnp.where(head_of == h, turned, jnp.zeros_like(turned)) for h in range(HEADS)], axis=1
+    )
+
+
+def stacks(count, key_tiles, tile, feats):
+    return [
+        pltpu.VMEM((count * key_tiles, feats, HEADS * tile), jnp.bfloat16),
+        pltpu.VMEM((count * key_tiles, HEADS * tile, feats), jnp.bfloat16),
+    ]
+
+
 def add_stop(n, tiles_ref, stop, keys, values, edges, query_ref, sums_ref, squares_ref, stack_ref, sizes):
     fibers, key_tiles, tile, scale = sizes
     capacity = tiles_ref.shape[-1]
     group = math.gcd(capacity, UNROLL)
     fiber = lax.axis_index("fiber")
-    tall = HEADS * tile
+    key_stack, value_stack = stack_ref
     lane = lax.broadcasted_iota(jnp.int32, (tile, LANES), 1)
     for c in range(key_tiles):
-        stack_ref[2 * n, c * tall : (c + 1) * tall, :] = head_masked(tile_of(keys, c, key_tiles * tile, tile, query_ref.shape[1]), HEADS)
-        stack_ref[2 * n + 1, c * tall : (c + 1) * tall, :] = head_masked(tile_of(values, c, key_tiles * tile, tile, query_ref.shape[1]), HEADS)
+        stack_keys(key_stack, n * key_tiles + c, tile_of(keys, c, key_tiles * tile, tile, query_ref.shape[1]))
+        value_stack[n * key_tiles + c] = head_masked(tile_of(values, c, key_tiles * tile, tile, query_ref.shape[1]), HEADS)
 
     def one_group(g, carry):
         for k in range(group):
@@ -110,12 +126,8 @@
             col_tile = lax.rem(number, key_tiles)
             part = lax.rem(lax.div(row_tile, key_tiles) - fiber + fibers, fibers)
             at = pl.multiple_of((part * key_tiles + lax.rem(row_tile, key_tiles)) * tile, tile)
-            stack = pl.ds(pl.multiple_of(col_tile * tall, tall), tall)
-            scores = lax.dot_general(
-                query_ref[pl.ds(at, tile), :],
-                stack_ref[2 * n, stack, :],
-                (((1,), (1,)), ((), ())),
-                preferred_element_type=jnp.float32,
+            scores = jnp.dot(
+                query_ref[pl.ds(at, tile), :], key_stack[n * key_tiles + col_tile], preferred_element_type=jnp.float32
             )
             edge_rows = pl.ds(edges[1] + slot * tile, tile)
             if not isinstance(slot, int):
@@ -129,7 +141,7 @@
                 den = jnp.where(lane == h, total, den)
             squares_ref[pl.ds(at, tile), :] += den
             sums_ref[pl.ds(at, tile), :] += jnp.dot(
-                weights.astype(jnp.bfloat16), stack_ref[2 * n + 1, stack, :], preferred_element_type=jnp.float32
+                weights.astype(jnp.bfloat16), value_stack[n * key_tiles + col_tile], preferred_element_type=jnp.float32
             )
         return carry
 
@@ -142,7 +154,7 @@
 def first_kernel(tiles_ref, *refs, plan, packets, sizes):
     fibers, key_tiles, tile, scale = sizes
     queries, arrived = refs[:fibers], refs[fibers : fibers + packets]
-    query_ref, sums_ref, squares_ref, stack_ref = refs[fibers + packets :]
+    query_ref, sums_ref, squares_ref, *stack_ref = refs[fibers + packets :]
     rows = key_tiles * tile
     for r in range(fibers):
         query_ref[r * rows : (r + 1) * rows, :] = queries[r][...]
@@ -158,24 +170,17 @@
         add_stop(n, tiles_ref, stop(core), *parts, query_ref, sums_ref, squares_ref, stack_ref, sizes)
 
 
-def more_kernel(tiles_ref, query_ref, sums_in, squares_in, *refs, plan, packets, sizes):
+def more_kernel(tiles_ref, query_ref, sums_in, squares_in, *refs, plan, packets, sizes, last):
     arrived = refs[:packets]
-    sums_ref, squares_ref, stack_ref = refs[packets:]
-    sums_ref[...] = sums_in[...]
-    squares_ref[...] = squares_in[...]
+    sums_ref, squares_ref, *stack_ref = refs[packets:]
+    if last:
+        payload_ref, *stack_ref = stack_ref
     add_plan(tiles_ref, plan, arrived, query_ref, sums_ref, squares_ref, stack_ref, sizes)
-
-
-def last_kernel(tiles_ref, query_ref, sums_in, squares_in, *refs, plan, packets, sizes):
-    arrived = refs[:packets]
-    num_ref, den_ref, payload_ref, stack_ref, sums_ref, squares_ref = refs[packets:]
-    sums_ref[...] = sums_in[...]
-    squares_ref[...] = squares_in[...]
-    add_plan(tiles_ref, plan, arrived, query_ref, sums_ref, squares_ref, stack_ref, sizes)
-    hand_out(sums_ref, squares_ref, num_ref, den_ref, payload_ref, sizes)
-
-
-def hand_out(sums_ref, squares_ref, num_ref, den_ref, payload_ref, sizes):
+    if last:
+        hand_out(sums_ref, squares_ref, payload_ref, sizes)
+
+
+def hand_out(sums_ref, squares_ref, payload_ref, sizes):
     fibers, key_tiles, tile, scale = sizes
     rows = key_tiles * tile
     half = EXTRA_ROWS // 2
@@ -187,14 +192,12 @@
             rest = den - high.astype(jnp.float32)
             both = jnp.concatenate([high.astype(jnp.float32).T[:half], rest.T[:half]], axis=0)
             payload_ref[r - 1, rows : rows + EXTRA_ROWS, t * tile : (t + 1) * tile] = both.astype(jnp.bfloat16)
-    num_ref[...] = sums_ref[:rows, :]
-    den_ref[...] = squares_ref[:rows, :]
 
 
 def finish_kernel(num_ref, den_ref, *refs, sizes):
     fibers, key_tiles, tile, scale = sizes
     *payloads, out_ref = refs
-    rows, feats = num_ref.shape
+    rows, feats = out_ref.shape
     head_dim = feats // HEADS
     half = EXTRA_ROWS // 2
     head_of = lax.broadcasted_iota(jnp.int32, (tile, feats), 1) // head_dim
@@ -247,50 +250,40 @@
         jax.ShapeDtypeStruct((fibers * rows, LANES), jnp.float32),
     ]
 
-    def stack(count):
-        return pltpu.VMEM((2 * count, key_tiles * HEADS * tile, feats), jnp.bfloat16)
-
     plan = [(lambda core: 0, (0, 0), (0, half_rows), (0, 2 * half_rows))]
     all_q, sums, squares = pl.pallas_call(
         functools.partial(first_kernel, plan=plan, packets=1, sizes=sizes),
         in_specs=[smem] + [WHOLE] * (1 + fibers),
         out_specs=[WHOLE] * 3,
         out_shape=state,
-        scratch_shapes=[stack(len(plan))],
+        scratch_shapes=stacks(len(plan), key_tiles, tile, feats),
         compiler_params=PARAMS,
         cost_estimate=SHORT,
     )(tiles, *all_queries, own)
     pairs, near, all_q, sums, squares = lax.optimization_barrier((pairs, near, all_q, sums, squares))
-    arrived, plan = [], []
+    far_packets, far_plan, near_packets, near_plan = [], [], [], []
     for s, pair, far_block, near_block in zip(shifts, pairs, far, near):
-        at = len(arrived)
-        arrived += [*far_block, pair, *near_block, routed(pair, lambda i: i ^ 1)]
-        plan.append((lambda core, s=s: s, (at, 0), (at + 1, 0), (at + 2, list_rows)))
-        plan.append((lambda core, s=s: jnp.where(core == 0, s - 1, s + 1), (at + 3, 0), (at + 4, 0), (at + 5, 0)))
-    sums, squares = pl.pallas_call(
-        functools.partial(more_kernel, plan=plan, packets=len(arrived), sizes=sizes),
-        in_specs=[smem] + [WHOLE] * (3 + len(arrived)),
-        out_specs=[WHOLE] * 2,
-        out_shape=state[1:],
-        scratch_shapes=[stack(len(plan))],
-        compiler_params=PARAMS,
-        cost_estimate=SHORT,
-    )(tiles, all_q, sums, squares, *arrived)
-    arrived = [odd]
-    plan = [(lambda core: jnp.where(core == 0, stops - 1, 1), (0, 0), (0, half_rows), (0, 2 * half_rows))]
-    num, den, payload = pl.pallas_call(
-        functools.partial(last_kernel, plan=plan, packets=len(arrived), sizes=sizes),
-        in_specs=[smem] + [WHOLE] * (3 + len(arrived)),
-        out_specs=[WHOLE] * 3,
-        out_shape=[
-            jax.ShapeDtypeStruct((rows, feats), jnp.float32),
-            jax.ShapeDtypeStruct((rows, LANES), jnp.float32),
-            jax.ShapeDtypeStruct((max(fibers - 1, 1), rows + EXTRA_ROWS, feats), jnp.bfloat16),
-        ],
-        scratch_shapes=[stack(len(plan)), pltpu.VMEM(state[1].shape, jnp.float32), pltpu.VMEM(state[2].shape, jnp.float32)],
-        compiler_params=PARAMS,
-        cost_estimate=SHORT,
-    )(tiles, all_q, sums, squares, *arrived)
+        at = len(far_packets)
+        far_packets += [*far_block, pair]
+        near_packets += [*near_block, routed(pair[:list_rows], lambda i: i ^ 1)]
+        far_plan.append((lambda core, s=s: s, (at, 0), (at + 1, 0), (at + 2, list_rows)))
+        near_plan.append((lambda core, s=s: jnp.where(core == 0, s - 1, s + 1), (at, 0), (at + 1, 0), (at + 2, 0)))
+    at = len(near_packets)
+    near_packets.append(odd)
+    near_plan.append((lambda core: jnp.where(core == 0, stops - 1, 1), (at, 0), (at, half_rows), (at, 2 * half_rows)))
+    for packets, plan, last in ((far_packets, far_plan, False), (near_packets, near_plan, True)):
+        sums, squares, *payload = pl.pallas_call(
+            functools.partial(more_kernel, plan=plan, packets=len(packets), sizes=sizes, last=last),
+            in_specs=[smem] + [WHOLE] * (3 + len(packets)),
+            out_specs=[WHOLE] * (2 + last),
+            out_shape=state[1:]
+            + [jax.ShapeDtypeStruct((max(fibers - 1, 1), rows + EXTRA_ROWS, feats), jnp.bfloat16)] * last,
+            input_output_aliases={2: 0, 3: 1},
+            scratch_shapes=stacks(len(plan), key_tiles, tile, feats),
+            compiler_params=PARAMS,
+            cost_estimate=SHORT,
+        )(tiles, all_q, sums, squares, *packets)
+    [payload] = payload
     partials = [moved(payload[r - 1], "fiber", r) for r in range(1, fibers)]
     return pl.pallas_call(
         functools.partial(finish_kernel, sizes=sizes),
@@ -299,7 +292,7 @@
         out_shape=jax.ShapeDtypeStruct((rows, feats), jnp.bfloat16),
         compiler_params=PARAMS,
         cost_estimate=SHORT,
-    )(num, den, *partials)
+    )(sums, squares, *partials)
 
 
 def solution(mesh):

time: 31.6 us -> 29.4 us (0.930)
  Pallas kernels: 8.26 us -> 6.81 us
  starting transfers between devices: 9.87 us -> 9.44 us
    ppermute x4, waiting for transfers between devices: 1.54 us -> 0.11 us  [routed(): lax.ppermute(block, 'blk', [(source_of(i) % count, i) for i in range(coun...]
    ppermute x5, waiting for transfers between devices: 11.7 us -> 12.9 us  [moved(): lax.ppermute(block, axis, [((i - distance) % count, i) for i in range(cou...]
    pallas_call x2, Pallas kernels: 4.21 us -> 3.14 us  [on_device(): pl.pallas_call(functools.partial(more_kernel, plan=plan, packets=len(pack...]
    ppermute x4, starting transfers between devices: 0.52 us -> 0.08 us  [routed(): lax.ppermute(block, 'blk', [(source_of(i) % count, i) for i in range(coun...]
    pallas_call x1, Pallas kernels: 1.67 us -> 1.3 us  [on_device(): pl.pallas_call(functools.partial(first_kernel, plan=plan, packets=1, size...]
  transfers between devices with their start and end apart: 9 -> 9, of which waited for: 5 -> 5; matrix products, arithmetic and copies ran while one was open for 0% -> 0% of each run, Pallas kernels for 18% -> 14%
where the time goes in v3:
time: 29.4 us; the launch traced here: 29.3 us
  waiting for transfers between devices  13 us (44%)
  starting transfers between devices  9.44 us (32%)
  Pallas kernels  6.81 us (23%)
    ppermute x5, waiting for transfers between devices, moved(): lax.ppermute(block, axis, [((i - distance) % count, i) for i in range(cou...  12.9 us
    ppermute x5, starting transfers between devices, moved(): lax.ppermute(block, axis, [((i - distance) % count, i) for i in range(cou...  9.37 us
    pallas_call x2, Pallas kernels, on_device(): pl.pallas_call(functools.partial(more_kernel, plan=plan, packets=len(pack...  3.14 us
    pallas_call x1, Pallas kernels, packed(): pl.pallas_call(functools.partial(pack_kernel, lists=lists), in_specs=[ANY...  1.42 us
    pallas_call x1, Pallas kernels, on_device(): pl.pallas_call(functools.partial(first_kernel, plan=plan, packets=1, size...  1.3 us
    pallas_call x1, Pallas kernels, on_device(): pl.pallas_call(functools.partial(finish_kernel, sizes=sizes), in_specs=[W...  0.96 us
  transfers between devices with their start and end apart: 9, of which 5 were waited for; matrix products, arithmetic and copies ran while one was open for 0% of the time, Pallas kernels for 14%

profile of v3, /device:TPU:0, one launch (start us, length us, event | category | flops | bytes accessed | tf_op | source)
XLA Modules:
  0.0 29.3 jit_solution(9333166283881730634)
XLA Ops:
  0.0 2.9 %collective-permute-start.1 = (bf16[256,256]{1,0:T(8,128)(2,1)}, bf16[256,256]{1,0:T(8,128)(2,1)S(1)}, u32[]{:S(2)}, u32[]{:S(2)}) collective-permute-start(bf16[256,256]{1,0:T(8,128)(2,1)} %key_ref.1), channel_id=1, source_target_pairs={{28,0},{30,2},{0,4},{2,6},{4,8},{6,10},{8,12},{10,14},{12,16},{14,... | collective-permute-start | bytes 393224 | tf_op jit(solution)/shard_map/ppermute | solution.py:26
  2.9 1.5 %collective-permute-start.3 = (bf16[256,256]{1,0:T(8,128)(2,1)}, bf16[256,256]{1,0:T(8,128)(2,1)S(1)}, u32[]{:S(2)}, u32[]{:S(2)}) collective-permute-start(bf16[256,256]{1,0:T(8,128)(2,1)} %value_ref.1), channel_id=1, source_target_pairs={{28,0},{30,2},{0,4},{2,6},{4,8},{6,10},{8,12},{10,14},{12,16},{14,... | collective-permute-start | bytes 393224 | tf_op jit(solution)/shard_map/ppermute | solution.py:26
  4.5 0.0 copy-start
  4.5 1.4 %shard_map.55 = (bf16[1536,128]{1,0:T(8,128)(2,1)S(1)}, bf16[1536,128]{1,0:T(8,128)(2,1)S(1)}, bf16[1024,128]{1,0:T(8,128)(2,1)S(1)}) custom-call(bf16[256,256]{1,0:T(8,128)(2,1)} %key_ref.1, bf16[256,256]{1,0:T(8,128)(2,1)} %value_ref.1, bf16[4,512,128]{2,1,0:T(8,128)(2,1)} %bitcast.3), custom_call_target="tpu_custom_call" | custom-call | flops 1 | bytes 1 | tf_op jit(solution)/shard_map/pallas_call | solution.py:67
  5.9 0.0 copy-start.1
  5.9 1.5 %collective-permute-start = (bf16[1024,128]{1,0:T(8,128)(2,1)S(1)}, bf16[1024,128]{1,0:T(8,128)(2,1)S(1)}, u32[]{:S(2)}, u32[]{:S(2)}) collective-permute-start(bf16[1024,128]{1,0:T(8,128)(2,1)S(1)} %get-tuple-element.22), channel_id=1, source_target_pairs={{28,0},{30,2},{0,4},{2,6},{4,8},{6,10},{8,12},{10,14},{12,16},{14,... | collective-permute-start | bytes 786440 | tf_op jit(solution)/shard_map/ppermute | solution.py:26
  7.5 0.0 collective-permute-start.7
  7.5 0.0 copy-done
  7.5 1.5 %collective-permute-start.5 = (bf16[256,256]{1,0:T(8,128)(2,1)S(1)}, bf16[256,256]{1,0:T(8,128)(2,1)S(1)}, u32[]{:S(2)}, u32[]{:S(2)}) collective-permute-start(bf16[256,256]{1,0:T(8,128)(2,1)S(1)} %copy-done), channel_id=1, source_target_pairs={{1,0},{0,1},{3,2},{2,3},{5,4},{4,5},{7,6},{6,7},{9,8},{8,9},{11,10... | collective-permute-start | bytes 393224 | tf_op jit(solution)/shard_map/ppermute | solution.py:26
  9.0 1.5 %collective-permute-done.1.refs_0_ = bf16[256,256]{1,0:T(8,128)(2,1)S(1)} collective-permute-done((bf16[256,256]{1,0:T(8,128)(2,1)}, bf16[256,256]{1,0:T(8,128)(2,1)S(1)}, u32[]{:S(2)}, u32[]{:S(2)}) %collective-permute-start.1) | collective-permute-done | bytes 131104 | tf_op jit(solution)/shard_map/ppermute | solution.py:26
  10.5 0.0 collective-permute-start.2
  10.5 2.8 %collective-permute-done.3.refs_1_ = bf16[256,256]{1,0:T(8,128)(2,1)S(1)} collective-permute-done((bf16[256,256]{1,0:T(8,128)(2,1)}, bf16[256,256]{1,0:T(8,128)(2,1)S(1)}, u32[]{:S(2)}, u32[]{:S(2)}) %collective-permute-start.3) | collective-permute-done | bytes 131104 | tf_op jit(solution)/shard_map/ppermute | solution.py:26
  13.3 0.0 collective-permute-start.4
  13.3 0.0 collective-permute-done.5.refs_1_
  13.3 0.0 copy-done.1
  13.3 1.3 %shard_map.56 = (bf16[512,256]{1,0:T(8,128)(2,1)S(1)}, f32[512,256]{1,0:T(8,128)S(1)}, f32[512,128]{1,0:T(8,128)S(1)}) custom-call(s32[1,1,4,4]{3,2,1,0:T(4,128)S(1)} %copy-done.1, bf16[256,256]{1,0:T(8,128)(2,1)S(1)} %copy-done, bf16[256,256]{1,0:T(8,128)(2,1)S(1)} %collective-permute-done.5.refs_1_, bf16[1536,128]{1,0:T(8,128)(2,1)S(1)} %get-tuple-element.23.refs_2_), custom_call_target="tpu_custom_call" | custom-call | flops 1 | bytes 1 | tf_op jit(solution)/shard_map/pallas_call | solution.py:254
  14.6 0.0 collective-permute-done.2.refs_0_
  14.6 0.0 collective-permute-done.4.refs_1_
  14.7 4.3 %collective-permute-done.refs_2_ = bf16[1024,128]{1,0:T(8,128)(2,1)S(1)} collective-permute-done((bf16[1024,128]{1,0:T(8,128)(2,1)S(1)}, bf16[1024,128]{1,0:T(8,128)(2,1)S(1)}, u32[]{:S(2)}, u32[]{:S(2)}) %collective-permute-start) | collective-permute-done | bytes 262176 | tf_op jit(solution)/shard_map/ppermute | solution.py:26
  18.9 0.1 collective-permute-start.6
  19.0 1.3 %shard_map.57 = (f32[512,256]{1,0:T(8,128)S(1)}, f32[512,128]{1,0:T(8,128)S(1)}) custom-call(s32[1,1,4,4]{3,2,1,0:T(4,128)S(1)} %copy-done.1, bf16[512,256]{1,0:T(8,128)(2,1)S(1)} %get-tuple-element.27.query_ref, f32[512,256]{1,0:T(8,128)S(1)} %get-tuple-element.28.sums_in, ...), custom_call_target="tpu_custom_call", output_to_operand_aliasing={{0}: (2, {}), {1}: (3, {})} | custom-call | flops 1 | bytes 1 | tf_op jit(solution)/shard_map/pallas_call | solution.py:275
  20.3 0.1 collective-permute-done.6.refs_2_
  20.4 0.0 collective-permute-done.7.refs_3_
  20.4 1.9 %shard_map.58 = (f32[512,256]{1,0:T(8,128)S(1)}, f32[512,128]{1,0:T(8,128)S(1)}, bf16[1,272,256]{2,1,0:T(8,128)(2,1)S(1)}) custom-call(s32[1,1,4,4]{3,2,1,0:T(4,128)S(1)} %copy-done.1, bf16[512,256]{1,0:T(8,128)(2,1)S(1)} %get-tuple-element.27.query_ref, f32[512,256]{1,0:T(8,128)S(1)} %get-tuple-element.31.sums_in, ...), custom_call_target="tpu_custom_call", output_to_operand_aliasing={{0}: (2, {}), {1}: (3, {})} | custom-call | flops 1 | bytes 1 | tf_op jit(solution)/shard_map/pallas_call | solution.py:275
  22.3 1.8 %collective-permute-start.8 = (bf16[272,256]{1,0:T(8,128)(2,1)S(1)}, bf16[272,256]{1,0:T(8,128)(2,1)S(1)}, u32[]{:S(2)}, u32[]{:S(2)}) collective-permute-start(bf16[272,256]{1,0:T(8,128)(2,1)S(1)} %bitcast.2), channel_id=1, source_target_pairs={{1,0},{0,1},{3,2},{2,3},{5,4},{4,5},{7,6},{6,7},{9,8},{8,9},{11,10... | collective-permute-start | bytes 417800 | tf_op jit(solution)/shard_map/ppermute | solution.py:26
  24.1 4.3 %collective-permute-done.8.refs_0_ = bf16[272,256]{1,0:T(8,128)(2,1)S(1)} collective-permute-done((bf16[272,256]{1,0:T(8,128)(2,1)S(1)}, bf16[272,256]{1,0:T(8,128)(2,1)S(1)}, u32[]{:S(2)}, u32[]{:S(2)}) %collective-permute-start.8) | collective-permute-done | bytes 139296 | tf_op jit(solution)/shard_map/ppermute | solution.py:26
  28.4 1.0 %shard_map.59 = bf16[256,256]{1,0:T(8,128)(2,1)} custom-call(f32[512,256]{1,0:T(8,128)S(1)} %get-tuple-element.36.num_ref, f32[512,128]{1,0:T(8,128)S(1)} %get-tuple-element.37.den_ref, bf16[272,256]{1,0:T(8,128)(2,1)S(1)} %collective-permute-done.8.refs_0_), custom_call_target="tpu_custom_call" | custom-call | flops 1 | bytes 1 | tf_op jit(solution)/shard_map/pallas_call | solution.py:288
  (1 shorter events, 0.0 us)
Async XLA Ops:
  0.0 10.5 %collective-permute-start.1 = (bf16[256,256]{1,0:T(8,128)(2,1)}, bf16[256,256]{1,0:T(8,128)(2,1)S(1)}, u32[]{:S(2)}, u32[]{:S(2)}) collective-permute-start(bf16[256,256]{1,0:T(8,128)(2,1)} %key_ref.1), channel_id=1, source_target_pairs={{28,0},{30,2},{0,4},{2,6},{4,8},{6,10},{8,12},{10,14},{12,16},{14,... | collective-permute-start | bytes 393224 | tf_op jit(solution)/shard_map/ppermute | solution.py:26
  2.9 10.4 %collective-permute-start.3 = (bf16[256,256]{1,0:T(8,128)(2,1)}, bf16[256,256]{1,0:T(8,128)(2,1)S(1)}, u32[]{:S(2)}, u32[]{:S(2)}) collective-permute-start(bf16[256,256]{1,0:T(8,128)(2,1)} %value_ref.1), channel_id=1, source_target_pairs={{28,0},{30,2},{0,4},{2,6},{4,8},{6,10},{8,12},{10,14},{12,16},{14,... | collective-permute-start | bytes 393224 | tf_op jit(solution)/shard_map/ppermute | solution.py:26
  4.5 3.0 %copy-start = (bf16[256,256]{1,0:T(8,128)(2,1)S(1)}, bf16[256,256]{1,0:T(8,128)(2,1)}, u32[]{:S(2)}) copy-start(bf16[256,256]{1,0:T(8,128)(2,1)} %refs_0_.1) | copy-start | bytes 393220
  5.9 7.4 %copy-start.1 = (s32[1,1,4,4]{3,2,1,0:T(4,128)S(1)}, s32[1,1,4,4]{3,2,1,0:T(4,128)}, u32[]{:S(2)}) copy-start(s32[1,1,4,4]{3,2,1,0:T(4,128)} %tiles_ref.5) | copy-start | bytes 196
  5.9 13.0 %collective-permute-start = (bf16[1024,128]{1,0:T(8,128)(2,1)S(1)}, bf16[1024,128]{1,0:T(8,128)(2,1)S(1)}, u32[]{:S(2)}, u32[]{:S(2)}) collective-permute-start(bf16[1024,128]{1,0:T(8,128)(2,1)S(1)} %get-tuple-element.22), channel_id=1, source_target_pairs={{28,0},{30,2},{0,4},{2,6},{4,8},{6,10},{8,12},{10,14},{12,16},{14,... | collective-permute-start | bytes 786440 | tf_op jit(solution)/shard_map/ppermute | solution.py:26
  7.5 12.9 %collective-permute-start.7 = (bf16[1536,128]{1,0:T(8,128)(2,1)S(1)}, bf16[1536,128]{1,0:T(8,128)(2,1)S(1)}, u32[]{:S(2)}, u32[]{:S(2)}) collective-permute-start(bf16[1536,128]{1,0:T(8,128)(2,1)S(1)} %get-tuple-element.35), channel_id=1, source_target_pairs={{26,0},{0,2},{30,4},{4,6},{2,8},{8,10},{6,12},{12,14},{10,16},{16,... | collective-permute-start | bytes 1179656 | tf_op jit(solution)/shard_map/ppermute | solution.py:31
  7.5 5.8 %collective-permute-start.5 = (bf16[256,256]{1,0:T(8,128)(2,1)S(1)}, bf16[256,256]{1,0:T(8,128)(2,1)S(1)}, u32[]{:S(2)}, u32[]{:S(2)}) collective-permute-start(bf16[256,256]{1,0:T(8,128)(2,1)S(1)} %copy-done), channel_id=1, source_target_pairs={{1,0},{0,1},{3,2},{2,3},{5,4},{4,5},{7,6},{6,7},{9,8},{8,9},{11,10... | collective-permute-start | bytes 393224 | tf_op jit(solution)/shard_map/ppermute | solution.py:26
  10.5 4.1 %collective-permute-start.2 = (bf16[256,256]{1,0:T(8,128)(2,1)S(1)}, bf16[256,256]{1,0:T(8,128)(2,1)S(1)}, u32[]{:S(2)}, u32[]{:S(2)}) collective-permute-start(bf16[256,256]{1,0:T(8,128)(2,1)S(1)} %collective-permute-done.1.refs_0_), channel_id=1, source_target_pairs={{2,0},{0,2},{6,4},{4,6},{10,8},{8,10},{14,12},{12,14},{18,16},{16,... | collective-permute-start | bytes 393224 | tf_op jit(solution)/shard_map/ppermute | solution.py:31
  13.3 1.3 %collective-permute-start.4 = (bf16[256,256]{1,0:T(8,128)(2,1)S(1)}, bf16[256,256]{1,0:T(8,128)(2,1)S(1)}, u32[]{:S(2)}, u32[]{:S(2)}) collective-permute-start(bf16[256,256]{1,0:T(8,128)(2,1)S(1)} %collective-permute-done.3.refs_1_), channel_id=1, source_target_pairs={{2,0},{0,2},{6,4},{4,6},{10,8},{8,10},{14,12},{12,14},{18,16},{16,... | collective-permute-start | bytes 393224 | tf_op jit(solution)/shard_map/ppermute | solution.py:31
  18.9 1.4 %collective-permute-start.6 = (bf16[512,128]{1,0:T(8,128)(2,1)S(1)}, bf16[512,128]{1,0:T(8,128)(2,1)S(1)}, u32[]{:S(2)}, u32[]{:S(2)}) collective-permute-start(bf16[512,128]{1,0:T(8,128)(2,1)S(1)} %slice.3), channel_id=1, source_target_pairs={{2,0},{0,2},{6,4},{4,6},{10,8},{8,10},{14,12},{12,14},{18,16},{16,... | collective-permute-start | bytes 393224 | tf_op jit(solution)/shard_map/ppermute | solution.py:31
  22.3 6.1 %collective-permute-start.8 = (bf16[272,256]{1,0:T(8,128)(2,1)S(1)}, bf16[272,256]{1,0:T(8,128)(2,1)S(1)}, u32[]{:S(2)}, u32[]{:S(2)}) collective-permute-start(bf16[272,256]{1,0:T(8,128)(2,1)S(1)} %bitcast.2), channel_id=1, source_target_pairs={{1,0},{0,1},{3,2},{2,3},{5,4},{4,5},{7,6},{6,7},{9,8},{8,9},{11,10... | collective-permute-start | bytes 417800 | tf_op jit(solution)/shard_map/ppermute | solution.py:26

commit v4 on v3

--- a/solution.py
+++ b/solution.py
@@ -14,7 +14,7 @@
 UNROLL = 4
 EXTRA_ROWS = 16
 LANES = 128
-VMEM_BYTES = 16 * 2**20
+VMEM_BYTES = 32 * 2**20
 WHOLE = pl.BlockSpec(memory_space=pltpu.VMEM)
 ANYWHERE = pl.BlockSpec(memory_space=pltpu.HBM)
 PARAMS = pltpu.CompilerParams(vmem_limit_bytes=VMEM_BYTES)
@@ -106,49 +106,128 @@
     ]
 
 
-def add_stop(n, tiles_ref, stop, keys, values, edges, query_ref, sums_ref, squares_ref, stack_ref, sizes):
+def entries(tiles_ref, stop, first, count, numbers):
+    bits = numbers.bit_length()
+    lists = tiles_ref[0, 0]
+    slot = lax.broadcasted_iota(jnp.int32, lists.shape, 1) - first
+    here = (lax.broadcasted_iota(jnp.int32, lists.shape, 0) == stop) & (slot >= 0) & (slot < count)
+    shift = jnp.where(here, slot * bits, 0)
+    together = jnp.sum(jnp.where(here, lax.shift_left(lists + 1, shift), 0))
+    return [(lax.shift_right_logical(together, k * bits) & ((1 << bits) - 1)) - 1 for k in range(count)]
+
+
+def place_of(listed, key_tiles, tile, fibers):
+    number = jnp.maximum(listed, 0)
+    row_tile = lax.div(number, key_tiles)
+    part = lax.rem(lax.div(row_tile, key_tiles) - lax.axis_index("fiber") + fibers, fibers)
+    at = pl.multiple_of((part * key_tiles + lax.rem(row_tile, key_tiles)) * tile, tile)
+    return at, lax.rem(number, key_tiles)
+
+
+def over_slots(tiles_ref, stop, sizes, one_slot):
     fibers, key_tiles, tile, scale = sizes
     capacity = tiles_ref.shape[-1]
     group = math.gcd(capacity, UNROLL)
-    fiber = lax.axis_index("fiber")
-    key_stack, value_stack = stack_ref
-    lane = lax.broadcasted_iota(jnp.int32, (tile, LANES), 1)
-    for c in range(key_tiles):
-        stack_keys(key_stack, n * key_tiles + c, tile_of(keys, c, key_tiles * tile, tile, query_ref.shape[1]))
-        value_stack[n * key_tiles + c] = head_masked(tile_of(values, c, key_tiles * tile, tile, query_ref.shape[1]), HEADS)
 
     def one_group(g, carry):
+        listed = entries(tiles_ref, stop, g * group, group, fibers * key_tiles * key_tiles)
         for k in range(group):
-            slot = g * group + k
-            listed = tiles_ref[0, 0, stop, slot]
-            number = jnp.maximum(listed, 0)
-            row_tile = lax.div(number, key_tiles)
-            col_tile = lax.rem(number, key_tiles)
-            part = lax.rem(lax.div(row_tile, key_tiles) - fiber + fibers, fibers)
-            at = pl.multiple_of((part * key_tiles + lax.rem(row_tile, key_tiles)) * tile, tile)
-            scores = jnp.dot(
-                query_ref[pl.ds(at, tile), :], key_stack[n * key_tiles + col_tile], preferred_element_type=jnp.float32
-            )
-            edge_rows = pl.ds(edges[1] + slot * tile, tile)
-            if not isinstance(slot, int):
-                edge_rows = pl.ds(pl.multiple_of(edges[1] + slot * tile, tile), tile)
-            edge = jnp.where(listed >= 0, edges[0][edge_rows, :].astype(jnp.float32) * scale, 0.0)
-            weights = jnp.maximum(scores, LEAKY_SLOPE * scores) * jnp.concatenate([edge] * HEADS, axis=1)
-            squared = weights * weights
-            den = jnp.zeros((tile, LANES), jnp.float32)
-            for h in range(HEADS):
-                total = jnp.sum(squared[:, h * tile : (h + 1) * tile], axis=1, keepdims=True)
-                den = jnp.where(lane == h, total, den)
-            squares_ref[pl.ds(at, tile), :] += den
-            sums_ref[pl.ds(at, tile), :] += jnp.dot(
-                weights.astype(jnp.bfloat16), value_stack[n * key_tiles + col_tile], preferred_element_type=jnp.float32
-            )
+            one_slot(g * group + k, listed[k])
         return carry
 
     if capacity == group:
         one_group(0, 0)
     else:
         lax.fori_loop(0, capacity // group, one_group, 0)
+
+
+def rows_of(first, slot, tile):
+    at = first + slot * tile
+    return pl.ds(at if isinstance(at, int) else pl.multiple_of(at, tile), tile)
+
+
+def stack_block(first, keys, values, key_stack, value_stack, sizes):
+    fibers, key_tiles, tile, scale = sizes
+    feats = value_stack.shape[2]
+    for c in range(key_tiles):
+        stack_keys(key_stack, first + c, tile_of(keys, c, key_tiles * tile, tile, feats))
+        value_stack[first + c] = head_masked(tile_of(values, c, key_tiles * tile, tile, feats), HEADS)
+
+
+def bent_scores(query_ref, at, key_stack):
+    scores = jnp.dot(query_ref[pl.ds(at, tile_rows(key_stack)), :], key_stack, preferred_element_type=jnp.float32)
+    return jnp.maximum(scores, LEAKY_SLOPE * scores)
+
+
+def tile_rows(key_stack):
+    return key_stack.shape[1] // HEADS
+
+
+def add_tile(bent, listed, at, edge, value_stack, sums_ref, squares_ref, scale):
+    tile = edge.shape[0]
+    lane = lax.broadcasted_iota(jnp.int32, (tile, LANES), 1)
+    edge = jnp.where(listed >= 0, edge.astype(jnp.float32) * scale, 0.0)
+    weights = bent * jnp.concatenate([edge] * HEADS, axis=1)
+    squared = weights * weights
+    den = jnp.zeros((tile, LANES), jnp.float32)
+    for h in range(HEADS):
+        total = jnp.sum(squared[:, h * tile : (h + 1) * tile], axis=1, keepdims=True)
+        den = jnp.where(lane == h, total, den)
+    squares_ref[pl.ds(at, tile), :] += den
+    sums_ref[pl.ds(at, tile), :] += jnp.dot(weights.astype(jnp.bfloat16), value_stack, preferred_element_type=jnp.float32)
+
+
+def add_plan(tiles_ref, plan, arrived, query_ref, sums_ref, squares_ref, stacks_, sizes):
+    fibers, key_tiles, tile, scale = sizes
+    key_stack, value_stack = stacks_
+    core = core_of_blk()
+    for n, (stop, *parts) in enumerate(plan):
+        keys, values, (edge_ref, edge_at) = [(arrived[packet], at) for packet, at in parts]
+        stack_block(n * key_tiles, keys, values, key_stack, value_stack, sizes)
+
+        def one_slot(slot, listed, n=n, edge_ref=edge_ref, edge_at=edge_at):
+            at, column = place_of(listed, key_tiles, tile, fibers)
+            bent = bent_scores(query_ref, at, key_stack[n * key_tiles + column])
+            edge = edge_ref[rows_of(edge_at, slot, tile), :]
+            add_tile(bent, listed, at, edge, value_stack[n * key_tiles + column], sums_ref, squares_ref, scale)
+
+        over_slots(tiles_ref, stop(core), sizes, one_slot)
+
+
+def ready_kernel(tiles_ref, query_ref, *refs, plan, packets, sizes):
+    fibers, key_tiles, tile, scale = sizes
+    arrived, (bent_ref, value_stack, key_stack) = refs[:packets], refs[packets:]
+    capacity = tiles_ref.shape[-1]
+    core = core_of_blk()
+    for n, (stop, *parts) in enumerate(plan):
+        keys, values = [(arrived[packet], at) for packet, at in parts]
+        stack_block(n * key_tiles, keys, values, key_stack, value_stack, sizes)
+
+        def one_slot(slot, listed, n=n):
+            at, column = place_of(listed, key_tiles, tile, fibers)
+            bent_ref[rows_of(n * capacity * tile, slot, tile), :] = bent_scores(
+                query_ref, at, key_stack[n * key_tiles + column]
+            )
+
+        over_slots(tiles_ref, stop(core), sizes, one_slot)
+
+
+def edge_kernel(tiles_ref, bent_ref, value_stack, sums_in, squares_in, *refs, plan, packets, sizes, last):
+    fibers, key_tiles, tile, scale = sizes
+    arrived, (sums_ref, squares_ref, *payload_ref) = refs[:packets], refs[packets:]
+    capacity = tiles_ref.shape[-1]
+    core = core_of_blk()
+    for stop, n, (packet, edge_at) in plan:
+
+        def one_slot(slot, listed, n=n, edge_ref=arrived[packet], edge_at=edge_at):
+            at, column = place_of(listed, key_tiles, tile, fibers)
+            bent = bent_ref[rows_of(n * capacity * tile, slot, tile), :]
+            edge = edge_ref[rows_of(edge_at, slot, tile), :]
+            add_tile(bent, listed, at, edge, value_stack[n * key_tiles + column], sums_ref, squares_ref, scale)
+
+        over_slots(tiles_ref, stop(core), sizes, one_slot)
+    if last:
+        hand_out(sums_ref, squares_ref, payload_ref[0], sizes)
 
 
 def first_kernel(tiles_ref, *refs, plan, packets, sizes):
@@ -163,21 +242,9 @@
     add_plan(tiles_ref, plan, arrived, query_ref, sums_ref, squares_ref, stack_ref, sizes)
 
 
-def add_plan(tiles_ref, plan, arrived, query_ref, sums_ref, squares_ref, stack_ref, sizes):
-    core = core_of_blk()
-    for n, (stop, *parts) in enumerate(plan):
-        parts = [(arrived[packet], at) for packet, at in parts]
-        add_stop(n, tiles_ref, stop(core), *parts, query_ref, sums_ref, squares_ref, stack_ref, sizes)
-
-
-def more_kernel(tiles_ref, query_ref, sums_in, squares_in, *refs, plan, packets, sizes, last):
-    arrived = refs[:packets]
+def more_kernel(tiles_ref, query_ref, sums_in, squares_in, *refs, plan, packets, sizes):
     sums_ref, squares_ref, *stack_ref = refs[packets:]
-    if last:
-        payload_ref, *stack_ref = stack_ref
-    add_plan(tiles_ref, plan, arrived, query_ref, sums_ref, squares_ref, stack_ref, sizes)
-    if last:
-        hand_out(sums_ref, squares_ref, payload_ref, sizes)
+    add_plan(tiles_ref, plan, refs[:packets], query_ref, sums_ref, squares_ref, stack_ref, sizes)
 
 
 def hand_out(sums_ref, squares_ref, payload_ref, sizes):
@@ -187,10 +254,9 @@
     for r in range(1, fibers):
         payload_ref[r - 1, :rows, :] = sums_ref[r * rows : (r + 1) * rows, :].astype(jnp.bfloat16)
         for t in range(key_tiles):
-            den = squares_ref[r * rows + t * tile : r * rows + (t + 1) * tile, :]
-            high = den.astype(jnp.bfloat16)
-            rest = den - high.astype(jnp.float32)
-            both = jnp.concatenate([high.astype(jnp.float32).T[:half], rest.T[:half]], axis=0)
+            den = squares_ref[r * rows + t * tile : r * rows + (t + 1) * tile, :].T[:half]
+            high = den.astype(jnp.bfloat16).astype(jnp.float32)
+            both = jnp.concatenate([high, den - high], axis=0)
             payload_ref[r - 1, rows : rows + EXTRA_ROWS, t * tile : (t + 1) * tile] = both.astype(jnp.bfloat16)
 
 
@@ -243,7 +309,6 @@
     odd = routed(odd, lambda i: i - 1 if i % CORES else i - stops + 1)
     all_queries = [queries] + [moved(queries, "fiber", -r) for r in range(1, fibers)]
 
-    smem = pl.BlockSpec(memory_space=pltpu.SMEM)
     state = [
         jax.ShapeDtypeStruct((fibers * rows, feats), jnp.bfloat16),
         jax.ShapeDtypeStruct((fibers * rows, feats), jnp.float32),
@@ -253,37 +318,62 @@
     plan = [(lambda core: 0, (0, 0), (0, half_rows), (0, 2 * half_rows))]
     all_q, sums, squares = pl.pallas_call(
         functools.partial(first_kernel, plan=plan, packets=1, sizes=sizes),
-        in_specs=[smem] + [WHOLE] * (1 + fibers),
+        in_specs=[WHOLE] * (2 + fibers),
         out_specs=[WHOLE] * 3,
         out_shape=state,
         scratch_shapes=stacks(len(plan), key_tiles, tile, feats),
         compiler_params=PARAMS,
         cost_estimate=SHORT,
     )(tiles, *all_queries, own)
-    pairs, near, all_q, sums, squares = lax.optimization_barrier((pairs, near, all_q, sums, squares))
-    far_packets, far_plan, near_packets, near_plan = [], [], [], []
-    for s, pair, far_block, near_block in zip(shifts, pairs, far, near):
-        at = len(far_packets)
-        far_packets += [*far_block, pair]
-        near_packets += [*near_block, routed(pair[:list_rows], lambda i: i ^ 1)]
-        far_plan.append((lambda core, s=s: s, (at, 0), (at + 1, 0), (at + 2, list_rows)))
-        near_plan.append((lambda core, s=s: jnp.where(core == 0, s - 1, s + 1), (at, 0), (at + 1, 0), (at + 2, 0)))
-    at = len(near_packets)
-    near_packets.append(odd)
-    near_plan.append((lambda core: jnp.where(core == 0, stops - 1, 1), (at, 0), (at, half_rows), (at, 2 * half_rows)))
-    for packets, plan, last in ((far_packets, far_plan, False), (near_packets, near_plan, True)):
-        sums, squares, *payload = pl.pallas_call(
-            functools.partial(more_kernel, plan=plan, packets=len(packets), sizes=sizes, last=last),
-            in_specs=[smem] + [WHOLE] * (3 + len(packets)),
+    ready_packets, ready_plan, far_plan, near_plan, cross = [], [], [], [], []
+    for n, (s, far_block, near_block) in enumerate(zip(shifts, far, near)):
+        of_far = lambda core, s=s: s
+        of_near = lambda core, s=s: jnp.where(core == 0, s - 1, s + 1)
+        ready_packets += [*far_block, *near_block]
+        ready_plan += [(of_far, (4 * n, 0), (4 * n + 1, 0)), (of_near, (4 * n + 2, 0), (4 * n + 3, 0))]
+        far_plan.append((of_far, 2 * n, (n, list_rows)))
+        near_plan.append((of_near, 2 * n + 1, (n, 0)))
+    lists_ready = len(ready_plan)
+    bent, value_stack = pl.pallas_call(
+        functools.partial(ready_kernel, plan=ready_plan, packets=len(ready_packets), sizes=sizes),
+        in_specs=[WHOLE] * (2 + len(ready_packets)),
+        out_specs=[WHOLE] * 2,
+        out_shape=[
+            jax.ShapeDtypeStruct((lists_ready * list_rows, HEADS * tile), jnp.float32),
+            jax.ShapeDtypeStruct((lists_ready * key_tiles, HEADS * tile, feats), jnp.bfloat16),
+        ],
+        scratch_shapes=stacks(lists_ready, key_tiles, tile, feats)[:1],
+        compiler_params=PARAMS,
+        cost_estimate=SHORT,
+    )(tiles, all_q, *ready_packets)
+    pairs, bent, value_stack, sums, squares = lax.optimization_barrier((pairs, bent, value_stack, sums, squares))
+    cross = [routed(pair[:list_rows], lambda i: i ^ 1) for pair in pairs]
+
+    def add_edges(packets, plan, sums, squares, last):
+        return pl.pallas_call(
+            functools.partial(edge_kernel, plan=plan, packets=len(packets), sizes=sizes, last=last),
+            in_specs=[WHOLE] * (5 + len(packets)),
             out_specs=[WHOLE] * (2 + last),
             out_shape=state[1:]
             + [jax.ShapeDtypeStruct((max(fibers - 1, 1), rows + EXTRA_ROWS, feats), jnp.bfloat16)] * last,
-            input_output_aliases={2: 0, 3: 1},
-            scratch_shapes=stacks(len(plan), key_tiles, tile, feats),
+            input_output_aliases={3: 0, 4: 1},
             compiler_params=PARAMS,
             cost_estimate=SHORT,
-        )(tiles, all_q, sums, squares, *packets)
-    [payload] = payload
+        )(tiles, bent, value_stack, sums, squares, *packets)
+
+    sums, squares = add_edges(pairs, far_plan, sums, squares, False)
+    odd_plan = [(lambda core: jnp.where(core == 0, stops - 1, 1), (0, 0), (0, half_rows), (0, 2 * half_rows))]
+    sums, squares = pl.pallas_call(
+        functools.partial(more_kernel, plan=odd_plan, packets=1, sizes=sizes),
+        in_specs=[WHOLE] * 5,
+        out_specs=[WHOLE] * 2,
+        out_shape=state[1:],
+        input_output_aliases={2: 0, 3: 1},
+        scratch_shapes=stacks(1, key_tiles, tile, feats),
+        compiler_params=PARAMS,
+        cost_estimate=SHORT,
+    )(tiles, all_q, sums, squares, odd)
+    sums, squares, payload = add_edges(cross, near_plan, sums, squares, True)
     partials = [moved(payload[r - 1], "fiber", r) for r in range(1, fibers)]
     return pl.pallas_call(
         functools.partial(finish_kernel, sizes=sizes),

time: 29.4 us -> 28.5 us (0.969)
  waiting for transfers between devices: 13 us -> 11.3 us
  local copies, waits for them, and re-layouts: 0.02 us -> 1.59 us
  Pallas kernels: 6.81 us -> 5.93 us
    ppermute x5, waiting for transfers between devices: 12.9 us -> 11.3 us  [moved(): lax.ppermute(block, axis, [((i - distance) % count, i) for i in range(cou...]
    unnamed x4, local copies, waits for them, and re-layouts: 0.01 us -> 1.59 us
    pallas_call x1, Pallas kernels: 1.3 us -> 0.72 us  [on_device(): pl.pallas_call(functools.partial(first_kernel, plan=plan, packets=1, size...]
    pallas_call x2 -> x4, Pallas kernels: 3.14 us -> 2.86 us  [the longest x2 1.44 us: add_edges(): pl.pallas_call(functools.partial(edge_kernel, plan=plan, packets=len(pack...]
  transfers between devices with their start and end apart: 9 -> 9, of which waited for: 5 -> 4; matrix products, arithmetic and copies ran while one was open for 0% -> 0% of each run, Pallas kernels for 14% -> 15%
where the time goes in v4:
time: 28.5 us; the launch traced here: 28.3 us
  waiting for transfers between devices  11.3 us (40%)
  starting transfers between devices  9.4 us (33%)
  Pallas kernels  5.93 us (21%)
  local copies, waits for them, and re-layouts  1.59 us (6%)
    ppermute x5, waiting for transfers between devices, moved(): lax.ppermute(block, axis, [((i - distance) % count, i) for i in range(cou...  11.3 us
    ppermute x5, starting transfers between devices, moved(): lax.ppermute(block, axis, [((i - distance) % count, i) for i in range(cou...  9.33 us
    unnamed x4, local copies, waits for them, and re-layouts  1.59 us
    pallas_call x2, Pallas kernels, add_edges(): pl.pallas_call(functools.partial(edge_kernel, plan=plan, packets=len(pack...  1.44 us
    pallas_call x1, Pallas kernels, packed(): pl.pallas_call(functools.partial(pack_kernel, lists=lists), in_specs=[ANY...  1.39 us
    pallas_call x1, Pallas kernels, on_device(): pl.pallas_call(functools.partial(finish_kernel, sizes=sizes), in_specs=[W...  0.96 us
    pallas_call x1, Pallas kernels, on_device(): pl.pallas_call(functools.partial(more_kernel, plan=odd_plan, packets=1, s...  0.72 us
    pallas_call x1, Pallas kernels, on_device(): pl.pallas_call(functools.partial(first_kernel, plan=plan, packets=1, size...  0.72 us
  transfers between devices with their start and end apart: 9, of which 4 were waited for; matrix products, arithmetic and copies ran while one was open for 0% of the time, Pallas kernels for 15%

profile of v4, /device:TPU:0, one launch (start us, length us, event | category | flops | bytes accessed | tf_op | source)
XLA Modules:
  0.0 28.3 jit_solution(17926250534007818930)
XLA Ops:
  0.0 2.9 %collective-permute-start.2 = (bf16[256,256]{1,0:T(8,128)(2,1)}, bf16[256,256]{1,0:T(8,128)(2,1)S(1)}, u32[]{:S(2)}, u32[]{:S(2)}) collective-permute-start(bf16[256,256]{1,0:T(8,128)(2,1)} %key_ref.1), channel_id=1, source_target_pairs={{28,0},{30,2},{0,4},{2,6},{4,8},{6,10},{8,12},{10,14},{12,16},{14,... | collective-permute-start | bytes 393224 | tf_op jit(solution)/shard_map/ppermute | solution.py:26
  2.9 1.5 %collective-permute-start.3 = (bf16[256,256]{1,0:T(8,128)(2,1)}, bf16[256,256]{1,0:T(8,128)(2,1)S(1)}, u32[]{:S(2)}, u32[]{:S(2)}) collective-permute-start(bf16[256,256]{1,0:T(8,128)(2,1)} %value_ref.1), channel_id=1, source_target_pairs={{28,0},{30,2},{0,4},{2,6},{4,8},{6,10},{8,12},{10,14},{12,16},{14,... | collective-permute-start | bytes 393224 | tf_op jit(solution)/shard_map/ppermute | solution.py:26
  4.5 1.4 %shard_map.55 = (bf16[1536,128]{1,0:T(8,128)(2,1)S(1)}, bf16[1536,128]{1,0:T(8,128)(2,1)S(1)}, bf16[1024,128]{1,0:T(8,128)(2,1)S(1)}) custom-call(bf16[256,256]{1,0:T(8,128)(2,1)} %key_ref.1, bf16[256,256]{1,0:T(8,128)(2,1)} %value_ref.1, bf16[4,512,128]{2,1,0:T(8,128)(2,1)} %bitcast.3), custom_call_target="tpu_custom_call" | custom-call | flops 1 | bytes 1 | tf_op jit(solution)/shard_map/pallas_call | solution.py:67
  5.9 1.5 %collective-permute-start = (bf16[1024,128]{1,0:T(8,128)(2,1)S(1)}, bf16[1024,128]{1,0:T(8,128)(2,1)S(1)}, u32[]{:S(2)}, u32[]{:S(2)}) collective-permute-start(bf16[1024,128]{1,0:T(8,128)(2,1)S(1)} %get-tuple-element.25), channel_id=1, source_target_pairs={{28,0},{30,2},{0,4},{2,6},{4,8},{6,10},{8,12},{10,14},{12,16},{14,... | collective-permute-start | bytes 786440 | tf_op jit(solution)/shard_map/ppermute | solution.py:26
  7.4 0.0 collective-permute-start.6
  7.4 1.5 %collective-permute-start.1 = (bf16[256,256]{1,0:T(8,128)(2,1)}, bf16[256,256]{1,0:T(8,128)(2,1)S(1)}, u32[]{:S(2)}, u32[]{:S(2)}) collective-permute-start(bf16[256,256]{1,0:T(8,128)(2,1)} %refs_0_.1), channel_id=1, source_target_pairs={{1,0},{0,1},{3,2},{2,3},{5,4},{4,5},{7,6},{6,7},{9,8},{8,9},{11,10... | collective-permute-start | bytes 393224 | tf_op jit(solution)/shard_map/ppermute | solution.py:26
  9.0 1.6 %collective-permute-done.2.refs_0_ = bf16[256,256]{1,0:T(8,128)(2,1)S(1)} collective-permute-done((bf16[256,256]{1,0:T(8,128)(2,1)}, bf16[256,256]{1,0:T(8,128)(2,1)S(1)}, u32[]{:S(2)}, u32[]{:S(2)}) %collective-permute-start.2) | collective-permute-done | bytes 131104 | tf_op jit(solution)/shard_map/ppermute | solution.py:26
  10.5 0.0 collective-permute-start.4
  10.5 2.8 %collective-permute-done.3.refs_1_ = bf16[256,256]{1,0:T(8,128)(2,1)S(1)} collective-permute-done((bf16[256,256]{1,0:T(8,128)(2,1)}, bf16[256,256]{1,0:T(8,128)(2,1)S(1)}, u32[]{:S(2)}, u32[]{:S(2)}) %collective-permute-start.3) | collective-permute-done | bytes 131104 | tf_op jit(solution)/shard_map/ppermute | solution.py:26
  13.3 0.0 collective-permute-start.5
  13.3 0.0 collective-permute-done.1.refs_1_
  13.3 0.0 copy-start
  13.3 0.9 %copy-done = bf16[256,256]{1,0:T(8,128)(2,1)S(1)} copy-done((bf16[256,256]{1,0:T(8,128)(2,1)S(1)}, bf16[256,256]{1,0:T(8,128)(2,1)}, u32[]{:S(2)}) %copy-start) | copy-done | bytes 131096
  14.2 0.0 copy-start.1
  14.2 0.7 %copy-done.1 = s32[1,1,4,4]{3,2,1,0:T(4,128)S(1)} copy-done((s32[1,1,4,4]{3,2,1,0:T(4,128)S(1)}, s32[1,1,4,4]{3,2,1,0:T(4,128)}, u32[]{:S(2)}) %copy-start.1) | copy-done | bytes 88
  14.9 0.7 %shard_map.56 = (bf16[512,256]{1,0:T(8,128)(2,1)S(1)}, f32[512,256]{1,0:T(8,128)S(1)}, f32[512,128]{1,0:T(8,128)S(1)}) custom-call(s32[1,1,4,4]{3,2,1,0:T(4,128)S(1)} %copy-done.1, bf16[256,256]{1,0:T(8,128)(2,1)S(1)} %copy-done, bf16[256,256]{1,0:T(8,128)(2,1)S(1)} %collective-permute-done.1.refs_1_, bf16[1536,128]{1,0:T(8,128)(2,1)S(1)} %get-tuple-element.26.refs_2_), custom_call_target="tpu_custom_call" | custom-call | flops 1 | bytes 1 | tf_op jit(solution)/shard_map/pallas_call | solution.py:319
  15.6 0.0 collective-permute-done.4.refs_2_
  15.7 0.0 collective-permute-done.5.refs_3_
  15.7 0.7 %shard_map.57 = (f32[1024,512]{1,0:T(8,128)S(1)}, bf16[4,512,256]{2,1,0:T(8,128)(2,1)S(1)}) custom-call(s32[1,1,4,4]{3,2,1,0:T(4,128)S(1)} %copy-done.1, bf16[512,256]{1,0:T(8,128)(2,1)S(1)} %get-tuple-element.27.query_ref, bf16[256,256]{1,0:T(8,128)(2,1)S(1)} %collective-permute-done.2.refs_0_, bf16[256,256]{1,0:T(8,128)(2,1)S(1)} %collective-permute-done.3.refs_1_, ...), custom_call_target="tpu_custom_call" | custom-call | flops 1 | bytes 1 | tf_op jit(solution)/shard_map/pallas_call | solution.py:337
  16.4 2.6 %collective-permute-done.refs_0_ = bf16[1024,128]{1,0:T(8,128)(2,1)S(1)} collective-permute-done((bf16[1024,128]{1,0:T(8,128)(2,1)S(1)}, bf16[1024,128]{1,0:T(8,128)(2,1)S(1)}, u32[]{:S(2)}, u32[]{:S(2)}) %collective-permute-start) | collective-permute-done | bytes 262176 | tf_op jit(solution)/shard_map/ppermute | solution.py:26
  18.9 0.1 collective-permute-start.7
  19.0 0.7 %shard_map.58 = (f32[512,256]{1,0:T(8,128)S(1)}, f32[512,128]{1,0:T(8,128)S(1)}) custom-call(s32[1,1,4,4]{3,2,1,0:T(4,128)S(1)} %copy-done.1, f32[1024,512]{1,0:T(8,128)S(1)} %get-tuple-element.32.bent_ref, bf16[4,512,256]{2,1,0:T(8,128)(2,1)S(1)} %get-tuple-element.33.value_stack, ...), custom_call_target="tpu_custom_call", output_to_operand_aliasing={{0}: (3, {}), {1}: (4, {})} | custom-call | flops 1 | bytes 1 | tf_op jit(solution)/shard_map/pallas_call | solution.py:353
  19.7 0.0 collective-permute-done.6.refs_0_
  19.7 0.7 %shard_map.59 = (f32[512,256]{1,0:T(8,128)S(1)}, f32[512,128]{1,0:T(8,128)S(1)}) custom-call(s32[1,1,4,4]{3,2,1,0:T(4,128)S(1)} %copy-done.1, bf16[512,256]{1,0:T(8,128)(2,1)S(1)} %get-tuple-element.27.query_ref, f32[512,256]{1,0:T(8,128)S(1)} %get-tuple-element.37.sums_in, ...), custom_call_target="tpu_custom_call", output_to_operand_aliasing={{0}: (2, {}), {1}: (3, {})} | custom-call | flops 1 | bytes 1 | tf_op jit(solution)/shard_map/pallas_call | solution.py:366
  20.4 0.0 collective-permute-done.7.refs_0_
  20.4 0.8 %shard_map.60 = (f32[512,256]{1,0:T(8,128)S(1)}, f32[512,128]{1,0:T(8,128)S(1)}, bf16[1,272,256]{2,1,0:T(8,128)(2,1)S(1)}) custom-call(s32[1,1,4,4]{3,2,1,0:T(4,128)S(1)} %copy-done.1, f32[1024,512]{1,0:T(8,128)S(1)} %get-tuple-element.32.bent_ref, ...), custom_call_target="tpu_custom_call", output_to_operand_aliasing={{0}: (3, {}), {1}: (4, {})} | custom-call | flops 1 | bytes 1 | tf_op jit(solution)/shard_map/pallas_call | solution.py:353
  21.2 1.8 %collective-permute-start.8 = (bf16[272,256]{1,0:T(8,128)(2,1)S(1)}, bf16[272,256]{1,0:T(8,128)(2,1)S(1)}, u32[]{:S(2)}, u32[]{:S(2)}) collective-permute-start(bf16[272,256]{1,0:T(8,128)(2,1)S(1)} %bitcast.2), channel_id=1, source_target_pairs={{1,0},{0,1},{3,2},{2,3},{5,4},{4,5},{7,6},{6,7},{9,8},{8,9},{11,10... | collective-permute-start | bytes 417800 | tf_op jit(solution)/shard_map/ppermute | solution.py:26
  23.0 4.3 %collective-permute-done.8.refs_0_ = bf16[272,256]{1,0:T(8,128)(2,1)S(1)} collective-permute-done((bf16[272,256]{1,0:T(8,128)(2,1)S(1)}, bf16[272,256]{1,0:T(8,128)(2,1)S(1)}, u32[]{:S(2)}, u32[]{:S(2)}) %collective-permute-start.8) | collective-permute-done | bytes 139296 | tf_op jit(solution)/shard_map/ppermute | solution.py:26
  27.3 1.0 %shard_map.61 = bf16[256,256]{1,0:T(8,128)(2,1)} custom-call(f32[512,256]{1,0:T(8,128)S(1)} %get-tuple-element.42.num_ref, f32[512,128]{1,0:T(8,128)S(1)} %get-tuple-element.43.den_ref, bf16[272,256]{1,0:T(8,128)(2,1)S(1)} %collective-permute-done.8.refs_0_), custom_call_target="tpu_custom_call" | custom-call | flops 1 | bytes 1 | tf_op jit(solution)/shard_map/pallas_call | solution.py:378
  (1 shorter events, 0.0 us)
Async XLA Ops:
  0.0 10.5 %collective-permute-start.2 = (bf16[256,256]{1,0:T(8,128)(2,1)}, bf16[256,256]{1,0:T(8,128)(2,1)S(1)}, u32[]{:S(2)}, u32[]{:S(2)}) collective-permute-start(bf16[256,256]{1,0:T(8,128)(2,1)} %key_ref.1), channel_id=1, source_target_pairs={{28,0},{30,2},{0,4},{2,6},{4,8},{6,10},{8,12},{10,14},{12,16},{14,... | collective-permute-start | bytes 393224 | tf_op jit(solution)/shard_map/ppermute | solution.py:26
  2.9 10.4 %collective-permute-start.3 = (bf16[256,256]{1,0:T(8,128)(2,1)}, bf16[256,256]{1,0:T(8,128)(2,1)S(1)}, u32[]{:S(2)}, u32[]{:S(2)}) collective-permute-start(bf16[256,256]{1,0:T(8,128)(2,1)} %value_ref.1), channel_id=1, source_target_pairs={{28,0},{30,2},{0,4},{2,6},{4,8},{6,10},{8,12},{10,14},{12,16},{14,... | collective-permute-start | bytes 393224 | tf_op jit(solution)/shard_map/ppermute | solution.py:26
  5.9 13.0 %collective-permute-start = (bf16[1024,128]{1,0:T(8,128)(2,1)S(1)}, bf16[1024,128]{1,0:T(8,128)(2,1)S(1)}, u32[]{:S(2)}, u32[]{:S(2)}) collective-permute-start(bf16[1024,128]{1,0:T(8,128)(2,1)S(1)} %get-tuple-element.25), channel_id=1, source_target_pairs={{28,0},{30,2},{0,4},{2,6},{4,8},{6,10},{8,12},{10,14},{12,16},{14,... | collective-permute-start | bytes 786440 | tf_op jit(solution)/shard_map/ppermute | solution.py:26
  7.4 12.3 %collective-permute-start.6 = (bf16[1536,128]{1,0:T(8,128)(2,1)S(1)}, bf16[1536,128]{1,0:T(8,128)(2,1)S(1)}, u32[]{:S(2)}, u32[]{:S(2)}) collective-permute-start(bf16[1536,128]{1,0:T(8,128)(2,1)S(1)} %get-tuple-element.39), channel_id=1, source_target_pairs={{26,0},{0,2},{30,4},{4,6},{2,8},{8,10},{6,12},{12,14},{10,16},{16,... | collective-permute-start | bytes 1179656 | tf_op jit(solution)/shard_map/ppermute | solution.py:31
  7.4 5.9 %collective-permute-start.1 = (bf16[256,256]{1,0:T(8,128)(2,1)}, bf16[256,256]{1,0:T(8,128)(2,1)S(1)}, u32[]{:S(2)}, u32[]{:S(2)}) collective-permute-start(bf16[256,256]{1,0:T(8,128)(2,1)} %refs_0_.1), channel_id=1, source_target_pairs={{1,0},{0,1},{3,2},{2,3},{5,4},{4,5},{7,6},{6,7},{9,8},{8,9},{11,10... | collective-permute-start | bytes 393224 | tf_op jit(solution)/shard_map/ppermute | solution.py:26
  10.5 5.1 %collective-permute-start.4 = (bf16[256,256]{1,0:T(8,128)(2,1)S(1)}, bf16[256,256]{1,0:T(8,128)(2,1)S(1)}, u32[]{:S(2)}, u32[]{:S(2)}) collective-permute-start(bf16[256,256]{1,0:T(8,128)(2,1)S(1)} %collective-permute-done.2.refs_0_), channel_id=1, source_target_pairs={{2,0},{0,2},{6,4},{4,6},{10,8},{8,10},{14,12},{12,14},{18,16},{16,... | collective-permute-start | bytes 393224 | tf_op jit(solution)/shard_map/ppermute | solution.py:31
  13.3 2.3 %collective-permute-start.5 = (bf16[256,256]{1,0:T(8,128)(2,1)S(1)}, bf16[256,256]{1,0:T(8,128)(2,1)S(1)}, u32[]{:S(2)}, u32[]{:S(2)}) collective-permute-start(bf16[256,256]{1,0:T(8,128)(2,1)S(1)} %collective-permute-done.3.refs_1_), channel_id=1, source_target_pairs={{2,0},{0,2},{6,4},{4,6},{10,8},{8,10},{14,12},{12,14},{18,16},{16,... | collective-permute-start | bytes 393224 | tf_op jit(solution)/shard_map/ppermute | solution.py:31
  13.3 0.9 %copy-start = (bf16[256,256]{1,0:T(8,128)(2,1)S(1)}, bf16[256,256]{1,0:T(8,128)(2,1)}, u32[]{:S(2)}) copy-start(bf16[256,256]{1,0:T(8,128)(2,1)} %refs_0_.1) | copy-start | bytes 393220
  14.2 0.7 %copy-start.1 = (s32[1,1,4,4]{3,2,1,0:T(4,128)S(1)}, s32[1,1,4,4]{3,2,1,0:T(4,128)}, u32[]{:S(2)}) copy-start(s32[1,1,4,4]{3,2,1,0:T(4,128)} %tiles_ref.9) | copy-start | bytes 196
  18.9 1.5 %collective-permute-start.7 = (bf16[512,128]{1,0:T(8,128)(2,1)S(1)}, bf16[512,128]{1,0:T(8,128)(2,1)S(1)}, u32[]{:S(2)}, u32[]{:S(2)}) collective-permute-start(bf16[512,128]{1,0:T(8,128)(2,1)S(1)} %slice.3), channel_id=1, source_target_pairs={{2,0},{0,2},{6,4},{4,6},{10,8},{8,10},{14,12},{12,14},{18,16},{16,... | collective-permute-start | bytes 393224 | tf_op jit(solution)/shard_map/ppermute | solution.py:31
  21.2 6.1 %collective-permute-start.8 = (bf16[272,256]{1,0:T(8,128)(2,1)S(1)}, bf16[272,256]{1,0:T(8,128)(2,1)S(1)}, u32[]{:S(2)}, u32[]{:S(2)}) collective-permute-start(bf16[272,256]{1,0:T(8,128)(2,1)S(1)} %bitcast.2), channel_id=1, source_target_pairs={{1,0},{0,1},{3,2},{2,3},{5,4},{4,5},{7,6},{6,7},{9,8},{8,9},{11,10... | collective-permute-start | bytes 417800 | tf_op jit(solution)/shard_map/ppermute | solution.py:26

commit v5 on v4

--- a/solution.py
+++ b/solution.py
@@ -124,21 +124,20 @@
     return at, lax.rem(number, key_tiles)
 
 
-def over_slots(tiles_ref, stop, sizes, one_slot):
+def over_groups(tiles_ref, stop, sizes, one_group):
     fibers, key_tiles, tile, scale = sizes
     capacity = tiles_ref.shape[-1]
     group = math.gcd(capacity, UNROLL)
 
-    def one_group(g, carry):
-        listed = entries(tiles_ref, stop, g * group, group, fibers * key_tiles * key_tiles)
-        for k in range(group):
-            one_slot(g * group + k, listed[k])
+    def step(g, carry):
+        first = g * group
+        one_group(first, entries(tiles_ref, stop, first, group, fibers * key_tiles * key_tiles))
         return carry
 
     if capacity == group:
-        one_group(0, 0)
+        step(0, 0)
     else:
-        lax.fori_loop(0, capacity // group, one_group, 0)
+        lax.fori_loop(0, capacity // group, step, 0)
 
 
 def rows_of(first, slot, tile):
@@ -163,18 +162,17 @@
     return key_stack.shape[1] // HEADS
 
 
-def add_tile(bent, listed, at, edge, value_stack, sums_ref, squares_ref, scale):
+def blended(bent, edge, value_stack, scale):
     tile = edge.shape[0]
     lane = lax.broadcasted_iota(jnp.int32, (tile, LANES), 1)
-    edge = jnp.where(listed >= 0, edge.astype(jnp.float32) * scale, 0.0)
+    edge = edge.astype(jnp.float32) * scale
     weights = bent * jnp.concatenate([edge] * HEADS, axis=1)
     squared = weights * weights
     den = jnp.zeros((tile, LANES), jnp.float32)
     for h in range(HEADS):
         total = jnp.sum(squared[:, h * tile : (h + 1) * tile], axis=1, keepdims=True)
         den = jnp.where(lane == h, total, den)
-    squares_ref[pl.ds(at, tile), :] += den
-    sums_ref[pl.ds(at, tile), :] += jnp.dot(weights.astype(jnp.bfloat16), value_stack, preferred_element_type=jnp.float32)
+    return jnp.dot(weights.astype(jnp.bfloat16), value_stack, preferred_element_type=jnp.float32), den
 
 
 def add_plan(tiles_ref, plan, arrived, query_ref, sums_ref, squares_ref, stacks_, sizes):
@@ -183,49 +181,59 @@
     core = core_of_blk()
     for n, (stop, *parts) in enumerate(plan):
         keys, values, (edge_ref, edge_at) = [(arrived[packet], at) for packet, at in parts]
+        capacity = tiles_ref.shape[-1]
+
+        def one_group(first, listed, n=n, edge_ref=edge_ref, edge_at=edge_at):
+            for k, number in enumerate(listed):
+                at, column = place_of(number, key_tiles, tile, fibers)
+                bent = bent_scores(query_ref, at, key_stack[n * key_tiles + column])
+                bent = jnp.where(number >= 0, bent, 0.0)
+                edge = edge_ref[rows_of(edge_at, first + k, tile), :]
+                num, den = blended(bent, edge, value_stack[n * key_tiles + column], scale)
+                squares_ref[pl.ds(at, tile), :] += den
+                sums_ref[pl.ds(at, tile), :] += num
+
         stack_block(n * key_tiles, keys, values, key_stack, value_stack, sizes)
-
-        def one_slot(slot, listed, n=n, edge_ref=edge_ref, edge_at=edge_at):
-            at, column = place_of(listed, key_tiles, tile, fibers)
-            bent = bent_scores(query_ref, at, key_stack[n * key_tiles + column])
-            edge = edge_ref[rows_of(edge_at, slot, tile), :]
-            add_tile(bent, listed, at, edge, value_stack[n * key_tiles + column], sums_ref, squares_ref, scale)
-
-        over_slots(tiles_ref, stop(core), sizes, one_slot)
+        over_groups(tiles_ref, stop(core), sizes, one_group)
 
 
 def ready_kernel(tiles_ref, query_ref, *refs, plan, packets, sizes):
     fibers, key_tiles, tile, scale = sizes
-    arrived, (bent_ref, value_stack, key_stack) = refs[:packets], refs[packets:]
+    arrived, (bent_ref, slot_values, key_stack, value_stack) = refs[:packets], refs[packets:]
     capacity = tiles_ref.shape[-1]
     core = core_of_blk()
     for n, (stop, *parts) in enumerate(plan):
         keys, values = [(arrived[packet], at) for packet, at in parts]
         stack_block(n * key_tiles, keys, values, key_stack, value_stack, sizes)
 
-        def one_slot(slot, listed, n=n):
-            at, column = place_of(listed, key_tiles, tile, fibers)
-            bent_ref[rows_of(n * capacity * tile, slot, tile), :] = bent_scores(
-                query_ref, at, key_stack[n * key_tiles + column]
-            )
-
-        over_slots(tiles_ref, stop(core), sizes, one_slot)
-
-
-def edge_kernel(tiles_ref, bent_ref, value_stack, sums_in, squares_in, *refs, plan, packets, sizes, last):
-    fibers, key_tiles, tile, scale = sizes
-    arrived, (sums_ref, squares_ref, *payload_ref) = refs[:packets], refs[packets:]
+        def one_group(first, listed, n=n):
+            for k, number in enumerate(listed):
+                at, column = place_of(number, key_tiles, tile, fibers)
+                bent = bent_scores(query_ref, at, key_stack[n * key_tiles + column])
+                bent_ref[rows_of(n * capacity * tile, first + k, tile), :] = jnp.where(number >= 0, bent, 0.0)
+                slot_values[n * capacity + first + k] = value_stack[n * key_tiles + column]
+
+        over_groups(tiles_ref, stop(core), sizes, one_group)
+
+
+def edge_kernel(tiles_ref, bent_ref, slot_values, sums_in, squares_in, *refs, plan, packets, sizes, last):
+    fibers, key_tiles, tile, scale = sizes
+    arrived, (sums_ref, squares_ref, *payload_ref, num_ref, den_ref) = refs[:packets], refs[packets:]
     capacity = tiles_ref.shape[-1]
     core = core_of_blk()
     for stop, n, (packet, edge_at) in plan:
 
-        def one_slot(slot, listed, n=n, edge_ref=arrived[packet], edge_at=edge_at):
-            at, column = place_of(listed, key_tiles, tile, fibers)
-            bent = bent_ref[rows_of(n * capacity * tile, slot, tile), :]
-            edge = edge_ref[rows_of(edge_at, slot, tile), :]
-            add_tile(bent, listed, at, edge, value_stack[n * key_tiles + column], sums_ref, squares_ref, scale)
-
-        over_slots(tiles_ref, stop(core), sizes, one_slot)
+        def one_group(first, listed, n=n, edge_ref=arrived[packet], edge_at=edge_at):
+            for k in range(len(listed)):
+                bent = bent_ref[rows_of(n * capacity * tile, first + k, tile), :]
+                edge = edge_ref[rows_of(edge_at, first + k, tile), :]
+                num_ref[n, k], den_ref[n, k] = blended(bent, edge, slot_values[n * capacity + first + k], scale)
+            for k, number in enumerate(listed):
+                at, _ = place_of(number, key_tiles, tile, fibers)
+                squares_ref[pl.ds(at, tile), :] += den_ref[n, k]
+                sums_ref[pl.ds(at, tile), :] += num_ref[n, k]
+
+        over_groups(tiles_ref, stop(core), sizes, one_group)
     if last:
         hand_out(sums_ref, squares_ref, payload_ref[0], sizes)
 
@@ -334,19 +342,19 @@
         far_plan.append((of_far, 2 * n, (n, list_rows)))
         near_plan.append((of_near, 2 * n + 1, (n, 0)))
     lists_ready = len(ready_plan)
-    bent, value_stack = pl.pallas_call(
+    bent, slot_values = pl.pallas_call(
         functools.partial(ready_kernel, plan=ready_plan, packets=len(ready_packets), sizes=sizes),
         in_specs=[WHOLE] * (2 + len(ready_packets)),
         out_specs=[WHOLE] * 2,
         out_shape=[
             jax.ShapeDtypeStruct((lists_ready * list_rows, HEADS * tile), jnp.float32),
-            jax.ShapeDtypeStruct((lists_ready * key_tiles, HEADS * tile, feats), jnp.bfloat16),
+            jax.ShapeDtypeStruct((lists_ready * capacity, HEADS * tile, feats), jnp.bfloat16),
         ],
-        scratch_shapes=stacks(lists_ready, key_tiles, tile, feats)[:1],
+        scratch_shapes=stacks(lists_ready, key_tiles, tile, feats),
         compiler_params=PARAMS,
         cost_estimate=SHORT,
     )(tiles, all_q, *ready_packets)
-    pairs, bent, value_stack, sums, squares = lax.optimization_barrier((pairs, bent, value_stack, sums, squares))
+    pairs, bent, slot_values, sums, squares = lax.optimization_barrier((pairs, bent, slot_values, sums, squares))
     cross = [routed(pair[:list_rows], lambda i: i ^ 1) for pair in pairs]
 
     def add_edges(packets, plan, sums, squares, last):
@@ -357,9 +365,12 @@
             out_shape=state[1:]
             + [jax.ShapeDtypeStruct((max(fibers - 1, 1), rows + EXTRA_ROWS, feats), jnp.bfloat16)] * last,
             input_output_aliases={3: 0, 4: 1},
+            scratch_shapes=[
+                pltpu.VMEM((lists_ready, math.gcd(capacity, UNROLL), tile, width), jnp.float32) for width in (feats, LANES)
+            ],
             compiler_params=PARAMS,
             cost_estimate=SHORT,
-        )(tiles, bent, value_stack, sums, squares, *packets)
+        )(tiles, bent, slot_values, sums, squares, *packets)
 
     sums, squares = add_edges(pairs, far_plan, sums, squares, False)
     odd_plan = [(lambda core: jnp.where(core == 0, stops - 1, 1), (0, 0), (0, half_rows), (0, 2 * half_rows))]

time: 28.5 us -> 28.2 us (0.989)
  no operation moved by 1% of the time
where the time goes in v5:
time: 28.2 us; the launch traced here: 28 us
  waiting for transfers between devices  11.2 us (40%)
  starting transfers between devices  9.42 us (33%)
  Pallas kernels  5.73 us (20%)
  local copies, waits for them, and re-layouts  1.59 us (6%)
    ppermute x5, waiting for transfers between devices, moved(): lax.ppermute(block, axis, [((i - distance) % count, i) for i in range(cou...  11.2 us
    ppermute x5, starting transfers between devices, moved(): lax.ppermute(block, axis, [((i - distance) % count, i) for i in range(cou...  9.34 us
    unnamed x4, local copies, waits for them, and re-layouts  1.59 us
    pallas_call x1, Pallas kernels, packed(): pl.pallas_call(functools.partial(pack_kernel, lists=lists), in_specs=[ANY...  1.39 us
    pallas_call x2, Pallas kernels, add_edges(): pl.pallas_call(functools.partial(edge_kernel, plan=plan, packets=len(pack...  1.17 us
    pallas_call x1, Pallas kernels, on_device(): pl.pallas_call(functools.partial(finish_kernel, sizes=sizes), in_specs=[W...  0.96 us
    pallas_call x1, Pallas kernels, on_device(): pl.pallas_call(functools.partial(ready_kernel, plan=ready_plan, packets=l...  0.77 us
    pallas_call x1, Pallas kernels, on_device(): pl.pallas_call(functools.partial(first_kernel, plan=plan, packets=1, size...  0.72 us
  transfers between devices with their start and end apart: 9, of which 4 were waited for; matrix products, arithmetic and copies ran while one was open for 0% of the time, Pallas kernels for 15%

profile of v5, /device:TPU:0, one launch (start us, length us, event | category | flops | bytes accessed | tf_op | source)
XLA Modules:
  0.0 28.0 jit_solution(14042096289065642976)
XLA Ops:
  0.0 2.9 %collective-permute-start.2 = (bf16[256,256]{1,0:T(8,128)(2,1)}, bf16[256,256]{1,0:T(8,128)(2,1)S(1)}, u32[]{:S(2)}, u32[]{:S(2)}) collective-permute-start(bf16[256,256]{1,0:T(8,128)(2,1)} %key_ref.1), channel_id=1, source_target_pairs={{28,0},{30,2},{0,4},{2,6},{4,8},{6,10},{8,12},{10,14},{12,16},{14,... | collective-permute-start | bytes 393224 | tf_op jit(solution)/shard_map/ppermute | solution.py:26
  2.9 1.5 %collective-permute-start.3 = (bf16[256,256]{1,0:T(8,128)(2,1)}, bf16[256,256]{1,0:T(8,128)(2,1)S(1)}, u32[]{:S(2)}, u32[]{:S(2)}) collective-permute-start(bf16[256,256]{1,0:T(8,128)(2,1)} %value_ref.1), channel_id=1, source_target_pairs={{28,0},{30,2},{0,4},{2,6},{4,8},{6,10},{8,12},{10,14},{12,16},{14,... | collective-permute-start | bytes 393224 | tf_op jit(solution)/shard_map/ppermute | solution.py:26
  4.5 1.4 %shard_map.55 = (bf16[1536,128]{1,0:T(8,128)(2,1)S(1)}, bf16[1536,128]{1,0:T(8,128)(2,1)S(1)}, bf16[1024,128]{1,0:T(8,128)(2,1)S(1)}) custom-call(bf16[256,256]{1,0:T(8,128)(2,1)} %key_ref.1, bf16[256,256]{1,0:T(8,128)(2,1)} %value_ref.1, bf16[4,512,128]{2,1,0:T(8,128)(2,1)} %bitcast.3), custom_call_target="tpu_custom_call" | custom-call | flops 1 | bytes 1 | tf_op jit(solution)/shard_map/pallas_call | solution.py:67
  5.9 1.5 %collective-permute-start = (bf16[1024,128]{1,0:T(8,128)(2,1)S(1)}, bf16[1024,128]{1,0:T(8,128)(2,1)S(1)}, u32[]{:S(2)}, u32[]{:S(2)}) collective-permute-start(bf16[1024,128]{1,0:T(8,128)(2,1)S(1)} %get-tuple-element.25), channel_id=1, source_target_pairs={{28,0},{30,2},{0,4},{2,6},{4,8},{6,10},{8,12},{10,14},{12,16},{14,... | collective-permute-start | bytes 786440 | tf_op jit(solution)/shard_map/ppermute | solution.py:26
  7.4 0.0 collective-permute-start.6
  7.4 1.5 %collective-permute-start.1 = (bf16[256,256]{1,0:T(8,128)(2,1)}, bf16[256,256]{1,0:T(8,128)(2,1)S(1)}, u32[]{:S(2)}, u32[]{:S(2)}) collective-permute-start(bf16[256,256]{1,0:T(8,128)(2,1)} %refs_0_.1), channel_id=1, source_target_pairs={{1,0},{0,1},{3,2},{2,3},{5,4},{4,5},{7,6},{6,7},{9,8},{8,9},{11,10... | collective-permute-start | bytes 393224 | tf_op jit(solution)/shard_map/ppermute | solution.py:26
  9.0 1.6 %collective-permute-done.2.refs_0_ = bf16[256,256]{1,0:T(8,128)(2,1)S(1)} collective-permute-done((bf16[256,256]{1,0:T(8,128)(2,1)}, bf16[256,256]{1,0:T(8,128)(2,1)S(1)}, u32[]{:S(2)}, u32[]{:S(2)}) %collective-permute-start.2) | collective-permute-done | bytes 131104 | tf_op jit(solution)/shard_map/ppermute | solution.py:26
  10.5 0.0 collective-permute-start.4
  10.5 2.8 %collective-permute-done.3.refs_1_ = bf16[256,256]{1,0:T(8,128)(2,1)S(1)} collective-permute-done((bf16[256,256]{1,0:T(8,128)(2,1)}, bf16[256,256]{1,0:T(8,128)(2,1)S(1)}, u32[]{:S(2)}, u32[]{:S(2)}) %collective-permute-start.3) | collective-permute-done | bytes 131104 | tf_op jit(solution)/shard_map/ppermute | solution.py:26
  13.3 0.0 collective-permute-start.5
  13.3 0.0 collective-permute-done.1.refs_1_
  13.3 0.0 copy-start
  13.3 0.9 %copy-done = bf16[256,256]{1,0:T(8,128)(2,1)S(1)} copy-done((bf16[256,256]{1,0:T(8,128)(2,1)S(1)}, bf16[256,256]{1,0:T(8,128)(2,1)}, u32[]{:S(2)}) %copy-start) | copy-done | bytes 131096
  14.2 0.0 copy-start.1
  14.2 0.7 %copy-done.1 = s32[1,1,4,4]{3,2,1,0:T(4,128)S(1)} copy-done((s32[1,1,4,4]{3,2,1,0:T(4,128)S(1)}, s32[1,1,4,4]{3,2,1,0:T(4,128)}, u32[]{:S(2)}) %copy-start.1) | copy-done | bytes 88
  14.9 0.7 %shard_map.56 = (bf16[512,256]{1,0:T(8,128)(2,1)S(1)}, f32[512,256]{1,0:T(8,128)S(1)}, f32[512,128]{1,0:T(8,128)S(1)}) custom-call(s32[1,1,4,4]{3,2,1,0:T(4,128)S(1)} %copy-done.1, bf16[256,256]{1,0:T(8,128)(2,1)S(1)} %copy-done, bf16[256,256]{1,0:T(8,128)(2,1)S(1)} %collective-permute-done.1.refs_1_, bf16[1536,128]{1,0:T(8,128)(2,1)S(1)} %get-tuple-element.26.refs_2_), custom_call_target="tpu_custom_call" | custom-call | flops 1 | bytes 1 | tf_op jit(solution)/shard_map/pallas_call | solution.py:327
  15.7 0.0 collective-permute-done.4.refs_2_
  15.7 0.0 collective-permute-done.5.refs_3_
  15.7 0.8 %shard_map.57 = (f32[1024,512]{1,0:T(8,128)S(1)}, bf16[8,512,256]{2,1,0:T(8,128)(2,1)S(1)}) custom-call(s32[1,1,4,4]{3,2,1,0:T(4,128)S(1)} %copy-done.1, bf16[512,256]{1,0:T(8,128)(2,1)S(1)} %get-tuple-element.27.query_ref, bf16[256,256]{1,0:T(8,128)(2,1)S(1)} %collective-permute-done.2.refs_0_, bf16[256,256]{1,0:T(8,128)(2,1)S(1)} %collective-permute-done.3.refs_1_, ...), custom_call_target="tpu_custom_call" | custom-call | flops 1 | bytes 1 | tf_op jit(solution)/shard_map/pallas_call | solution.py:345
  16.5 2.5 %collective-permute-done.refs_0_ = bf16[1024,128]{1,0:T(8,128)(2,1)S(1)} collective-permute-done((bf16[1024,128]{1,0:T(8,128)(2,1)S(1)}, bf16[1024,128]{1,0:T(8,128)(2,1)S(1)}, u32[]{:S(2)}, u32[]{:S(2)}) %collective-permute-start) | collective-permute-done | bytes 262176 | tf_op jit(solution)/shard_map/ppermute | solution.py:26
  18.9 0.1 collective-permute-start.7
  19.0 0.6 %shard_map.58 = (f32[512,256]{1,0:T(8,128)S(1)}, f32[512,128]{1,0:T(8,128)S(1)}) custom-call(s32[1,1,4,4]{3,2,1,0:T(4,128)S(1)} %copy-done.1, f32[1024,512]{1,0:T(8,128)S(1)} %get-tuple-element.32.bent_ref, bf16[8,512,256]{2,1,0:T(8,128)(2,1)S(1)} %get-tuple-element.33.slot_values, ...), custom_call_target="tpu_custom_call", output_to_operand_aliasing={{0}: (3, {}), {1}: (4, {})} | custom-call | flops 1 | bytes 1 | tf_op jit(solution)/shard_map/pallas_call | solution.py:361
  19.6 0.0 collective-permute-done.6.refs_0_
  19.6 0.7 %shard_map.59 = (f32[512,256]{1,0:T(8,128)S(1)}, f32[512,128]{1,0:T(8,128)S(1)}) custom-call(s32[1,1,4,4]{3,2,1,0:T(4,128)S(1)} %copy-done.1, bf16[512,256]{1,0:T(8,128)(2,1)S(1)} %get-tuple-element.27.query_ref, f32[512,256]{1,0:T(8,128)S(1)} %get-tuple-element.37.sums_in, ...), custom_call_target="tpu_custom_call", output_to_operand_aliasing={{0}: (2, {}), {1}: (3, {})} | custom-call | flops 1 | bytes 1 | tf_op jit(solution)/shard_map/pallas_call | solution.py:377
  20.3 0.0 collective-permute-done.7.refs_0_
  20.4 0.6 %shard_map.60 = (f32[512,256]{1,0:T(8,128)S(1)}, f32[512,128]{1,0:T(8,128)S(1)}, bf16[1,272,256]{2,1,0:T(8,128)(2,1)S(1)}) custom-call(s32[1,1,4,4]{3,2,1,0:T(4,128)S(1)} %copy-done.1, f32[1024,512]{1,0:T(8,128)S(1)} %get-tuple-element.32.bent_ref, ...), custom_call_target="tpu_custom_call", output_to_operand_aliasing={{0}: (3, {}), {1}: (4, {})} | custom-call | flops 1 | bytes 1 | tf_op jit(solution)/shard_map/pallas_call | solution.py:361
  21.0 1.8 %collective-permute-start.8 = (bf16[272,256]{1,0:T(8,128)(2,1)S(1)}, bf16[272,256]{1,0:T(8,128)(2,1)S(1)}, u32[]{:S(2)}, u32[]{:S(2)}) collective-permute-start(bf16[272,256]{1,0:T(8,128)(2,1)S(1)} %bitcast.2), channel_id=1, source_target_pairs={{1,0},{0,1},{3,2},{2,3},{5,4},{4,5},{7,6},{6,7},{9,8},{8,9},{11,10... | collective-permute-start | bytes 417800 | tf_op jit(solution)/shard_map/ppermute | solution.py:26
  22.8 4.3 %collective-permute-done.8.refs_0_ = bf16[272,256]{1,0:T(8,128)(2,1)S(1)} collective-permute-done((bf16[272,256]{1,0:T(8,128)(2,1)S(1)}, bf16[272,256]{1,0:T(8,128)(2,1)S(1)}, u32[]{:S(2)}, u32[]{:S(2)}) %collective-permute-start.8) | collective-permute-done | bytes 139296 | tf_op jit(solution)/shard_map/ppermute | solution.py:26
  27.1 1.0 %shard_map.61 = bf16[256,256]{1,0:T(8,128)(2,1)} custom-call(f32[512,256]{1,0:T(8,128)S(1)} %get-tuple-element.42.num_ref, f32[512,128]{1,0:T(8,128)S(1)} %get-tuple-element.43.den_ref, bf16[272,256]{1,0:T(8,128)(2,1)S(1)} %collective-permute-done.8.refs_0_), custom_call_target="tpu_custom_call" | custom-call | flops 1 | bytes 1 | tf_op jit(solution)/shard_map/pallas_call | solution.py:389
  (1 shorter events, 0.0 us)
Async XLA Ops:
  0.0 10.5 %collective-permute-start.2 = (bf16[256,256]{1,0:T(8,128)(2,1)}, bf16[256,256]{1,0:T(8,128)(2,1)S(1)}, u32[]{:S(2)}, u32[]{:S(2)}) collective-permute-start(bf16[256,256]{1,0:T(8,128)(2,1)} %key_ref.1), channel_id=1, source_target_pairs={{28,0},{30,2},{0,4},{2,6},{4,8},{6,10},{8,12},{10,14},{12,16},{14,... | collective-permute-start | bytes 393224 | tf_op jit(solution)/shard_map/ppermute | solution.py:26
  2.9 10.4 %collective-permute-start.3 = (bf16[256,256]{1,0:T(8,128)(2,1)}, bf16[256,256]{1,0:T(8,128)(2,1)S(1)}, u32[]{:S(2)}, u32[]{:S(2)}) collective-permute-start(bf16[256,256]{1,0:T(8,128)(2,1)} %value_ref.1), channel_id=1, source_target_pairs={{28,0},{30,2},{0,4},{2,6},{4,8},{6,10},{8,12},{10,14},{12,16},{14,... | collective-permute-start | bytes 393224 | tf_op jit(solution)/shard_map/ppermute | solution.py:26
  5.9 13.0 %collective-permute-start = (bf16[1024,128]{1,0:T(8,128)(2,1)S(1)}, bf16[1024,128]{1,0:T(8,128)(2,1)S(1)}, u32[]{:S(2)}, u32[]{:S(2)}) collective-permute-start(bf16[1024,128]{1,0:T(8,128)(2,1)S(1)} %get-tuple-element.25), channel_id=1, source_target_pairs={{28,0},{30,2},{0,4},{2,6},{4,8},{6,10},{8,12},{10,14},{12,16},{14,... | collective-permute-start | bytes 786440 | tf_op jit(solution)/shard_map/ppermute | solution.py:26
  7.4 12.2 %collective-permute-start.6 = (bf16[1536,128]{1,0:T(8,128)(2,1)S(1)}, bf16[1536,128]{1,0:T(8,128)(2,1)S(1)}, u32[]{:S(2)}, u32[]{:S(2)}) collective-permute-start(bf16[1536,128]{1,0:T(8,128)(2,1)S(1)} %get-tuple-element.39), channel_id=1, source_target_pairs={{26,0},{0,2},{30,4},{4,6},{2,8},{8,10},{6,12},{12,14},{10,16},{16,... | collective-permute-start | bytes 1179656 | tf_op jit(solution)/shard_map/ppermute | solution.py:31
  7.4 5.9 %collective-permute-start.1 = (bf16[256,256]{1,0:T(8,128)(2,1)}, bf16[256,256]{1,0:T(8,128)(2,1)S(1)}, u32[]{:S(2)}, u32[]{:S(2)}) collective-permute-start(bf16[256,256]{1,0:T(8,128)(2,1)} %refs_0_.1), channel_id=1, source_target_pairs={{1,0},{0,1},{3,2},{2,3},{5,4},{4,5},{7,6},{6,7},{9,8},{8,9},{11,10... | collective-permute-start | bytes 393224 | tf_op jit(solution)/shard_map/ppermute | solution.py:26
  10.5 5.1 %collective-permute-start.4 = (bf16[256,256]{1,0:T(8,128)(2,1)S(1)}, bf16[256,256]{1,0:T(8,128)(2,1)S(1)}, u32[]{:S(2)}, u32[]{:S(2)}) collective-permute-start(bf16[256,256]{1,0:T(8,128)(2,1)S(1)} %collective-permute-done.2.refs_0_), channel_id=1, source_target_pairs={{2,0},{0,2},{6,4},{4,6},{10,8},{8,10},{14,12},{12,14},{18,16},{16,... | collective-permute-start | bytes 393224 | tf_op jit(solution)/shard_map/ppermute | solution.py:31
  13.3 2.3 %collective-permute-start.5 = (bf16[256,256]{1,0:T(8,128)(2,1)S(1)}, bf16[256,256]{1,0:T(8,128)(2,1)S(1)}, u32[]{:S(2)}, u32[]{:S(2)}) collective-permute-start(bf16[256,256]{1,0:T(8,128)(2,1)S(1)} %collective-permute-done.3.refs_1_), channel_id=1, source_target_pairs={{2,0},{0,2},{6,4},{4,6},{10,8},{8,10},{14,12},{12,14},{18,16},{16,... | collective-permute-start | bytes 393224 | tf_op jit(solution)/shard_map/ppermute | solution.py:31
  13.3 0.9 %copy-start = (bf16[256,256]{1,0:T(8,128)(2,1)S(1)}, bf16[256,256]{1,0:T(8,128)(2,1)}, u32[]{:S(2)}) copy-start(bf16[256,256]{1,0:T(8,128)(2,1)} %refs_0_.1) | copy-start | bytes 393220
  14.2 0.7 %copy-start.1 = (s32[1,1,4,4]{3,2,1,0:T(4,128)S(1)}, s32[1,1,4,4]{3,2,1,0:T(4,128)}, u32[]{:S(2)}) copy-start(s32[1,1,4,4]{3,2,1,0:T(4,128)} %tiles_ref.9) | copy-start | bytes 196
  18.9 1.4 %collective-permute-start.7 = (bf16[512,128]{1,0:T(8,128)(2,1)S(1)}, bf16[512,128]{1,0:T(8,128)(2,1)S(1)}, u32[]{:S(2)}, u32[]{:S(2)}) collective-permute-start(bf16[512,128]{1,0:T(8,128)(2,1)S(1)} %slice.3), channel_id=1, source_target_pairs={{2,0},{0,2},{6,4},{4,6},{10,8},{8,10},{14,12},{12,14},{18,16},{16,... | collective-permute-start | bytes 393224 | tf_op jit(solution)/shard_map/ppermute | solution.py:31
  21.0 6.1 %collective-permute-start.8 = (bf16[272,256]{1,0:T(8,128)(2,1)S(1)}, bf16[272,256]{1,0:T(8,128)(2,1)S(1)}, u32[]{:S(2)}, u32[]{:S(2)}) collective-permute-start(bf16[272,256]{1,0:T(8,128)(2,1)S(1)} %bitcast.2), channel_id=1, source_target_pairs={{1,0},{0,1},{3,2},{2,3},{5,4},{4,5},{7,6},{6,7},{9,8},{8,9},{11,10... | collective-permute-start | bytes 417800 | tf_op jit(solution)/shard_map/ppermute | solution.py:26
